TPU v7x, 32 devices: a whole 2x2x4 slice. The times are simulated.
32 devices in a mesh: site: 4 (over z), fault: 8 (over y, x, core).
Axes of the slice: x: 2, y: 2, z: 4, core: 2. Of those that a mesh axis runs over, the one named last changes fastest.
Arguments:
- green_tensor: bfloat16 [4, 128, 96, 6, 256], P('site', 'fault'), may hold values from -0.375 to 0.375
- slip_map: bfloat16 [128, 8, 256], P('fault', None, 'site'), may hold values from 0.19921875 to 2
- rupture_time: float32 [128, 8, 256], P('fault', None, 'site'), may hold values from 0 to 48
- variation_ids: int32 [128, 8], P('fault'), may hold values from 0 to 7, each once within a row
- variation_count: int32 [128], P('fault'), may hold values from 2 to 8, as said below
- tile_rupture: int32 [128], P('fault'), may hold values from 0 to 7
- owner_slot: int32 [8], replicated, may hold values from 0 to 7, each once
Outputs:
- seismograms: float32 [8, 8, 4, 3, 192], P('fault', None, 'site')
Inputs may be any that keep to these rules, and one draw needn't show every extreme that they name: `variation_count`: every tile lists at least 2 of the 8 variations, and in every draw some tile lists all 8.
All inputs are finite; a program needn't handle non-finite values.
Results may differ from a plain program's by a relative error of at most 0.0027.
Values sent between devices are 32-bit elements; how exact they have to be, the bound alone decides.
A program may use at most 64 MiB of HBM per device.

v0:
```python
import math

import jax
import jax.numpy as jnp
from jax import lax
from jax.sharding import PartitionSpec as P


def inverse_table(freq_count):
    sample_count = 2 * freq_count
    wave = jnp.arange(freq_count, dtype=jnp.int32)[:, None]
    sample = jnp.arange(sample_count, dtype=jnp.int32)[None, :]
    angles = 2.0 * math.pi / sample_count * (wave * sample % sample_count).astype(jnp.float32)
    return jnp.concatenate([jnp.cos(angles), -jnp.sin(angles)], axis=0) / math.sqrt(freq_count)


def tile_terms(amplitude, arrival, green_tile):
    freq_count = green_tile.shape[-3]
    frequency = jnp.arange(freq_count, dtype=jnp.float32)
    phases = (
        2.0 * math.pi / (2 * freq_count) * frequency[:, None, None] * jnp.expand_dims(arrival, -3)
    )
    amplitude_wide = jnp.expand_dims(amplitude, -3)
    a_real = (amplitude_wide * jnp.cos(phases)).astype(jnp.bfloat16)
    a_imag = (-amplitude_wide * jnp.sin(phases)).astype(jnp.bfloat16)
    part_real = jnp.einsum(
        "...fvp,...fkp->...vkf", a_real, green_tile, preferred_element_type=jnp.float32
    )
    part_imag = jnp.einsum(
        "...fvp,...fkp->...vkf", a_imag, green_tile, preferred_element_type=jnp.float32
    )
    flat_shape = part_real.shape[:-2] + (part_real.shape[-2] * part_real.shape[-1],)
    return jnp.stack([part_real.reshape(flat_shape), part_imag.reshape(flat_shape)], axis=-3)


def per_device(
    green_tensor, slip_map, rupture_time, variation_ids, variation_count, tile_rupture, owner_slot
):
    green_tiles = green_tensor[0]
    tile_total = green_tiles.shape[0]
    freq_count = green_tiles.shape[1]
    row_count = slip_map.shape[1]
    amplitude_local = slip_map.astype(jnp.float32)
    amplitude_piece = lax.all_gather(amplitude_local, "site", axis=2, tiled=True)
    arrival_piece = lax.all_gather(rupture_time, "site", axis=2, tiled=True)
    running = tile_terms(amplitude_piece, arrival_piece, green_tiles)
    split = running.reshape(tile_total, 2, row_count, 6, freq_count)
    real_part = split[:, 0, :, :3] - split[:, 1, :, 3:]
    imag_part = split[:, 0, :, 3:] + split[:, 1, :, :3]
    spectrum = jnp.concatenate([real_part, imag_part], axis=-1).reshape(tile_total, row_count, -1)
    is_live = jnp.arange(row_count, dtype=jnp.int32)[None, :] < variation_count[:, None]
    selector = (
        (variation_ids[:, None, :] == jnp.arange(row_count, dtype=jnp.int32)[None, :, None])
        & is_live[:, None, :]
    ).astype(jnp.float32)
    ordered = jnp.einsum("tvj,tjx->tvx", selector, spectrum, precision=lax.Precision.HIGHEST)
    rupture_total = owner_slot.shape[0]
    member = (tile_rupture[:, None] == jnp.arange(rupture_total, dtype=jnp.int32)[None, :]).astype(
        jnp.int32
    )
    slot_index = jnp.sum(member * owner_slot[None, :], axis=1)
    route = (slot_index[None, :] == jnp.arange(rupture_total, dtype=jnp.int32)[:, None]).astype(
        jnp.float32
    )
    local_sum = jnp.dot(
        route,
        ordered.reshape(tile_total, -1),
        precision=lax.Precision.HIGHEST,
        preferred_element_type=jnp.float32,
    )
    received = lax.all_to_all(local_sum, "fault", split_axis=0, concat_axis=0, tiled=True)
    devices = lax.axis_size("fault")
    owned_sum = jnp.sum(received.reshape(devices, rupture_total // devices, -1), axis=0)
    owned_rows = owned_sum.shape[0]
    table = inverse_table(freq_count)
    seismic = jnp.dot(
        owned_sum.reshape(-1, 2 * freq_count),
        table,
        precision=lax.Precision.HIGHEST,
        preferred_element_type=jnp.float32,
    )
    return seismic.reshape(owned_rows, row_count, 1, 3, 2 * freq_count)


def solution(mesh):
    placed = (
        P("site", "fault", None, None, None),
        P("fault", None, "site"),
        P("fault", None, "site"),
        P("fault", None),
        P("fault"),
        P("fault"),
        P(),
    )
    return jax.shard_map(
        per_device,
        mesh=mesh,
        in_specs=placed,
        out_specs=P("fault", None, "site", None, None),
        check_vma=False,
    )
```

profile of v0, /device:TPU:0, one launch (start us, length us, event | category | flops | bytes accessed | tf_op | source)
XLA Modules:
  0.0 160.3 jit_solution(2655102888655329747)
XLA Ops:
  0.0 0.9 copy.45
  0.9 24.2 %all_gather.6 = f32[16,8,256]{0,1,2:T(8,128)S(1)} all-gather(f32[16,8,64]{0,1,2:T(8,128)S(1)} %copy.45), channel_id=1, replica_groups=mesh['site'=4,'fault'=8] {'site'}, dimensions={2}, use_global_device_ids=true | all-gather | bytes 163840 | tf_op jit(solution)/shard_map/all_gather | solution.py:44
  25.1 0.4 copy.46
  25.5 1.0 copy.47
  26.5 21.8 %all_gather.7 = f32[16,8,256]{0,1,2:T(8,128)S(1)} all-gather(f32[16,8,64]{0,1,2:T(8,128)S(1)} %copy.47), channel_id=1, replica_groups=mesh['site'=4,'fault'=8] {'site'}, dimensions={2}, use_global_device_ids=true | all-gather | bytes 163840 | tf_op jit(solution)/shard_map/all_gather | solution.py:45
  48.3 0.4 copy.48
  48.7 43.4 %fusion.18 = f32[16,1,8,6,96]{2,3,4,0,1:T(8,128)S(1)} fusion(bf16[16,96,6,256]{3,1,2,0:T(8,128)(2,1)} %bitcast.24, f32[16,8,256]{2,1,0:T(8,128)S(1)} %copy.48, f32[96]{0:T(128)S(1)} %iota_multiply_fusion, f32[16,8,256]{2,1,0:T(8,128)S(1)} %copy.46), kind=kOutput, calls=%fused_computation.22 | convolution fusion | flops 47185920 | bytes 5276032 | tf_op jit(solution)/shard_map/...fvp,...fkp->...vkf/dot_general | solution.py:26
  92.1 43.9 %fusion.23 = f32[16,1,8,6,96]{2,3,4,0,1:T(8,128)S(1)} fusion(bf16[16,96,6,256]{3,1,2,0:T(8,128)(2,1)} %bitcast.25, f32[16,8,256]{2,1,0:T(8,128)S(1)} %neg.7, f32[16,8,256]{2,1,0:T(8,128)S(1)} %copy.48, f32[96]{0:T(128)S(1)} %iota_multiply_fusion), kind=kOutput, calls=%fused_computation.23 | convolution fusion | flops 47185920 | bytes 5276032 | tf_op jit(solution)/shard_map/...fvp,...fkp->...vkf/dot_general | solution.py:29
  136.0 1.7 %fusion.17 = (f32[16,8,3,96]{1,2,3,0:T(4,128)S(1)}, f32[16,8,3,96]{1,2,3,0:T(4,128)S(1)}) fusion(f32[16,1,8,6,96]{2,3,4,0,1:T(8,128)S(1)} %fusion.23, f32[16,1,8,6,96]{2,3,4,0,1:T(8,128)S(1)} %fusion.18), kind=kLoop, calls=%fused_computation.21 | loop fusion | flops 73728 | bytes 884736 | tf_op jit(solution)/shard_map/sub | solution.py:48
  137.6 4.5 %pad_maximum_fusion = f32[16,8,3,192]{1,2,3,0:T(4,128)} fusion(f32[16,8,3,96]{1,2,3,0:T(4,128)S(1)} %get-tuple-element.6, f32[16,8,3,96]{1,2,3,0:T(4,128)S(1)} %get-tuple-element.5), kind=kLoop, calls=%fused_computation.10 | loop fusion | flops 73728 | bytes 589824 | tf_op jit(solution)/shard_map/concatenate | solution.py:50
  142.1 0.0 copy-start
  142.1 0.0 copy-start.1
  142.1 0.0 copy-start.2
  142.1 0.0 copy-start.3
  142.1 5.7 %copy.52 = f32[16,8,3,192]{3,2,1,0:T(4,128)S(1)} copy(f32[16,8,3,192]{1,2,3,0:T(4,128)} %pad_maximum_fusion) | data formatting | bytes 589824 | tf_op jit(solution)/shard_map/concatenate | solution.py:50
  147.8 0.3 reshape.58
  148.1 0.0 copy-done
  148.1 0.1 copy.44
  148.2 0.0 copy-done.1
  148.2 0.1 iota_compare_fusion.1
  148.3 0.3 fusion.40
  148.6 0.1 reshape.59
  148.7 0.0 copy-done.2
  148.7 0.0 copy-done.3
  148.7 0.1 select_reduce_fusion
  148.8 0.2 convolution_bitcast_fusion
  149.0 0.8 copy.53
  149.8 3.7 %all-to-all-start = ((f32[8,1,4608]{2,1,0:T(1,128)}), f32[8,1,4608]{2,1,0:T(1,128)S(1)}, u32[]{:S(2)}, u32[]{:S(2)}) async-start(f32[8,1,4608]{2,1,0:T(1,128)} %copy.53), calls=%async_computation | async-start | bytes 294912 | tf_op jit(solution)/shard_map/all_to_all | solution.py:71
  153.5 0.4 sine_negate_fusion
  154.0 5.3 %all-to-all-done = f32[8,1,4608]{2,1,0:T(1,128)S(1)} async-done(((f32[8,1,4608]{2,1,0:T(1,128)}), f32[8,1,4608]{2,1,0:T(1,128)S(1)}, u32[]{:S(2)}, u32[]{:S(2)}) %all-to-all-start) | async-done | bytes 147488 | tf_op jit(solution)/shard_map/all_to_all | solution.py:71
  159.3 0.1 reduce_sum.19
  159.4 0.1 reshape.60
  159.5 0.2 convolution_bitcast_fusion.1
  159.7 0.6 copy.55
  (2 shorter events, 0.0 us)
Async XLA Ops:
  142.1 6.0 %copy-start = (s32[16,8]{0,1:T(8,128)S(1)}, s32[16,8]{0,1:T(8,128)}, u32[]{:S(2)}) copy-start(s32[16,8]{0,1:T(8,128)} %param.10) | copy-start | bytes 1540
  142.1 6.1 %copy-start.1 = (s32[16]{0:T(128)S(1)}, s32[16]{0:T(128)}, u32[]{:S(2)}) copy-start(s32[16]{0:T(128)} %param.11) | copy-start | bytes 196
  142.1 6.6 %copy-start.2 = (s32[8]{0:T(128)S(1)}, s32[8]{0:T(128)}, u32[]{:S(2)}) copy-start(s32[8]{0:T(128)} %param.13) | copy-start | bytes 100
  142.1 6.6 %copy-start.3 = (s32[16]{0:T(128)S(1)}, s32[16]{0:T(128)}, u32[]{:S(2)}) copy-start(s32[16]{0:T(128)} %param.12) | copy-start | bytes 196
  149.8 9.4 %all-to-all-start = ((f32[8,1,4608]{2,1,0:T(1,128)}), f32[8,1,4608]{2,1,0:T(1,128)S(1)}, u32[]{:S(2)}, u32[]{:S(2)}) async-start(f32[8,1,4608]{2,1,0:T(1,128)} %copy.53), calls=%async_computation | async-start | bytes 294912 | tf_op jit(solution)/shard_map/all_to_all | solution.py:71
where the time goes:
time: 161 us; the launch traced here: 160 us
  matrix products  88 us (55%)
  blocking collectives  46 us (29%)
  local copies, waits for them, and re-layouts  10.3 us (6%)
  other arithmetic  6.86 us (4%)
  waiting for transfers between devices  5.29 us (3%)
  starting transfers between devices  3.72 us (2%)
    dot_general x1, matrix products, tile_terms(): jnp.einsum('...fvp,...fkp->...vkf', a_imag, green_tile, preferred_element...  43.9 us
    dot_general x1, matrix products, tile_terms(): jnp.einsum('...fvp,...fkp->...vkf', a_real, green_tile, preferred_element...  43.4 us
    all_gather x1, blocking collectives, per_device(): lax.all_gather(amplitude_local, 'site', axis=2, tiled=True)  24.2 us
    all_gather x1, blocking collectives, per_device(): arrival_piece = lax.all_gather(rupture_time, 'site', axis=2, tiled=True)  21.8 us
    concatenate x1, local copies, waits for them, and re-layouts, per_device(): jnp.concatenate([real_part, imag_part], axis=-1)  5.7 us
    all_to_all x1, waiting for transfers between devices, per_device(): lax.all_to_all(local_sum, 'fault', split_axis=0, concat_axis=0, tiled=True)  5.29 us
    concatenate x1, other arithmetic, per_device(): jnp.concatenate([real_part, imag_part], axis=-1)  4.47 us
    all_to_all x1, starting transfers between devices, per_device(): lax.all_to_all(local_sum, 'fault', split_axis=0, concat_axis=0, tiled=True)  3.72 us
  transfers between devices with their start and end apart: 1, of which 1 were waited for; matrix products, arithmetic and copies ran while one was open for 0% of the time, Pallas kernels for 0%

commit v1 on v0

v1 whole, which is shorter than its diff:
```python
import functools
import math

import jax
import jax.numpy as jnp
from jax import lax
from jax.experimental import pallas as pl
from jax.experimental.pallas import tpu as pltpu
from jax.sharding import PartitionSpec as P

BLOCK = 32
HALF = 8


def inverse_table(freq_count):
    sample_count = 2 * freq_count
    wave = jnp.arange(freq_count, dtype=jnp.int32)[:, None]
    sample = jnp.arange(sample_count, dtype=jnp.int32)[None, :]
    angles = 2.0 * math.pi / sample_count * (wave * sample % sample_count).astype(jnp.float32)
    return jnp.concatenate([jnp.cos(angles), -jnp.sin(angles)], axis=0) / math.sqrt(freq_count)


def cos_sin(angle):
    x = angle - math.pi / 4
    y = x * x
    c = jnp.float32(1.0)
    s = jnp.float32(1.0)
    for n in (5, 4, 3, 2, 1):
        c = 1.0 - y * (c * (1.0 / ((2 * n - 1) * (2 * n))))
        s = 1.0 - y * (s * (1.0 / ((2 * n) * (2 * n + 1))))
    s = s * x
    root = math.sqrt(0.5)
    return root * (c - s), root * (c + s)


def turn(a, b):
    return a[0] * b[0] - a[1] * b[1], a[0] * b[1] + a[1] * b[0]


def phasor_blocks(amplitude, arrival, freq_count, write):
    one = cos_sin(arrival * (2.0 * math.pi / (2 * freq_count)))
    one = (one[0], -one[1])
    powers = [None, one]
    for n in range(2, HALF + 1):
        powers.append(turn(powers[n // 2], powers[n - n // 2]))
    step = turn(powers[HALF], powers[HALF])
    centre = (amplitude * powers[HALF][0], amplitude * powers[HALF][1])
    for k in range(HALF, freq_count, 2 * HALF):
        write(k, *centre)
        for n in range(1, HALF + 1):
            cc, ss = centre[0] * powers[n][0], centre[1] * powers[n][1]
            cs, sc = centre[0] * powers[n][1], centre[1] * powers[n][0]
            write(k - n, cc + ss, sc - cs)
            if n < HALF:
                write(k + n, cc - ss, sc + cs)
        if k + 2 * HALF < freq_count:
            centre = turn(centre, step)


def compute_tile(tile, amplitude, arrival, green, phasor, spectrum):
    rows, points = amplitude.shape
    freq_count = green.shape[2]
    lanes = 4 * BLOCK
    for start in range(0, points, lanes):
        piece = slice(start, start + lanes)

        def write(k, real, imag):
            both = jnp.concatenate([real, imag], axis=0).astype(jnp.bfloat16)
            phasor[k * 2 * rows : (k + 1) * 2 * rows, piece] = both

        phasor_blocks(amplitude[:, piece], arrival[:, piece], freq_count, write)
    lane = lax.broadcasted_iota(jnp.int32, (2 * rows, 2 * lanes), 1) % BLOCK
    for block in range(freq_count // BLOCK):
        own = pl.ds(block * BLOCK, BLOCK)
        weights = jnp.concatenate([green[tile, c, own, :] for c in (0, 1, 2, 2, 3, 4, 5, 5)], axis=0)
        left = phasor[block * BLOCK * 2 * rows : (block + 1) * BLOCK * 2 * rows, :]
        product = lax.dot_general(
            left, weights, (((1,), (1,)), ((), ())), preferred_element_type=jnp.float32
        )
        picked = product[: 2 * rows]
        for k in range(1, BLOCK):
            picked = jnp.where(lane == k, product[k * 2 * rows : (k + 1) * 2 * rows], picked)
        real = picked[:rows, :lanes] - picked[rows:, lanes:]
        imag = picked[:rows, lanes:] + picked[rows:, :lanes]
        target = pl.ds(pl.multiple_of(tile * rows, rows), rows)
        spectrum[target, pl.ds(2 * block * lanes, lanes)] = real
        spectrum[target, pl.ds((2 * block + 1) * lanes, lanes)] = imag


def route_rows(ids, count, rupture, owner, spectrum, row_count, rupture_total):
    tile_total = ids.shape[1]
    wide = row_count * rupture_total
    column = lax.broadcasted_iota(jnp.int32, (row_count, wide), 1)
    slot = lax.broadcasted_iota(jnp.int32, (row_count, 1), 0)
    pieces = []
    for tile in range(tile_total):
        place = owner[rupture[tile]] * row_count
        target = jnp.where(slot < count[tile], ids[:, tile : tile + 1] + place, -1)
        pieces.append((column == target).astype(jnp.float32))
    member = jnp.concatenate(pieces, axis=0).astype(jnp.bfloat16)
    value = spectrum[...]
    high = value.astype(jnp.bfloat16)
    low = (value - high.astype(jnp.float32)).astype(jnp.bfloat16)
    dims = (((0,), (0,)), ((), ()))
    return lax.dot_general(
        jnp.concatenate([member, member], axis=0),
        jnp.concatenate([high, low], axis=0),
        dims,
        preferred_element_type=jnp.float32,
    )


def kernel(ids, count, rupture, owner, amplitude, arrival, green_hbm, out, green, phasor, spectrum, sems):
    tile_total, rows, _ = amplitude.shape
    for tile in range(tile_total):
        pltpu.make_async_copy(green_hbm.at[tile], green.at[tile], sems.at[tile]).start()

    def one(tile, carry):
        pltpu.make_async_copy(green_hbm.at[tile], green.at[tile], sems.at[tile]).wait()
        compute_tile(tile, amplitude[tile], arrival[tile], green, phasor, spectrum)
        return carry

    lax.fori_loop(0, tile_total, one, 0)
    out[...] = route_rows(ids, count, rupture, owner, spectrum, rows, owner.shape[0])


def per_device(
    green_tensor, slip_map, rupture_time, variation_ids, variation_count, tile_rupture, owner_slot
):
    green = jnp.swapaxes(green_tensor[0], 1, 2)
    tile_total, _, freq_count, points = green.shape
    rows = slip_map.shape[1]
    rupture_total = owner_slot.shape[0]
    local = jnp.concatenate([slip_map.astype(jnp.float32), rupture_time], axis=1)
    maps = lax.all_gather(local, "site", axis=2, tiled=True)
    width = 8 * freq_count
    smem = pl.BlockSpec(memory_space=pltpu.SMEM)
    vmem = pl.BlockSpec(memory_space=pltpu.VMEM)
    local_sum = pl.pallas_call(
        kernel,
        out_shape=jax.ShapeDtypeStruct((rupture_total * rows, width), jnp.float32),
        in_specs=[vmem, smem, smem, smem, vmem, vmem, pl.BlockSpec(memory_space=pl.ANY)],
        out_specs=vmem,
        scratch_shapes=[
            pltpu.VMEM(green.shape, jnp.bfloat16),
            pltpu.VMEM((freq_count * 2 * rows, points), jnp.bfloat16),
            pltpu.VMEM((tile_total * rows, width), jnp.float32),
            pltpu.SemaphoreType.DMA((tile_total,)),
        ],
        compiler_params=pltpu.CompilerParams(vmem_limit_bytes=40 * 1024 * 1024),
        cost_estimate=pl.CostEstimate(flops=2 * 10**9, bytes_accessed=5 * 10**6, transcendentals=0),
    )(
        variation_ids.T, variation_count, tile_rupture, owner_slot,
        maps[:, :rows], maps[:, rows:], green,
    )
    blocks = freq_count // BLOCK
    packed = local_sum.reshape(rupture_total, rows, blocks, 2, 4, BLOCK)[:, :, :, :, :3]
    packed = packed.reshape(rupture_total, -1)
    received = lax.all_to_all(packed, "fault", split_axis=0, concat_axis=0, tiled=True)
    devices = lax.axis_size("fault")
    owned = jnp.sum(received.reshape(devices, rupture_total // devices, -1), axis=0)
    owned = owned.reshape(-1, rows, blocks, 2, 3, BLOCK)
    owned = owned.transpose(0, 1, 4, 3, 2, 5).reshape(-1, 2 * freq_count)
    seismic = jnp.dot(
        owned,
        inverse_table(freq_count),
        precision=lax.Precision.HIGHEST,
        preferred_element_type=jnp.float32,
    )
    return seismic.reshape(rupture_total // devices, rows, 1, 3, 2 * freq_count)


def solution(mesh):
    placed = (
        P("site", "fault", None, None, None),
        P("fault", None, "site"),
        P("fault", None, "site"),
        P("fault", None),
        P("fault"),
        P("fault"),
        P(),
    )
    return jax.shard_map(
        per_device,
        mesh=mesh,
        in_specs=placed,
        out_specs=P("fault", None, "site", None, None),
        check_vma=False,
    )
```

time: 161 us -> 71.3 us (0.44)
  matrix products: 88 us -> 0.19 us
  Pallas kernels: 0 us -> 9.2 us
  blocking collectives: 46 us -> 39.7 us
  other arithmetic: 6.86 us -> 2.14 us
    dot_general x5 -> x1, matrix products: 88 us -> 0.19 us  [per_device(): jnp.dot(owned, inverse_table(freq_count), precision=lax.Precision.HIGHEST...]
    pallas_call x0 -> x1, Pallas kernels: none -> 9.2 us  [per_device(): pl.pallas_call(kernel, out_shape=jax.ShapeDtypeStruct((rupture_total * ro...]
    all_gather x2 -> x1, blocking collectives: 46 us -> 39.7 us  [per_device(): maps = lax.all_gather(local, 'site', axis=2, tiled=True)]
    concatenate x1, local copies, waits for them, and re-layouts: 5.7 us -> 0.28 us  [per_device(): jnp.concatenate([slip_map.astype(jnp.float32), rupture_time], axis=1)]
    unnamed x10 -> x12, local copies, waits for them, and re-layouts: 1.08 us -> 5.88 us
    concatenate x1, other arithmetic: 4.47 us -> 0.85 us  [per_device(): jnp.concatenate([slip_map.astype(jnp.float32), rupture_time], axis=1)]
    slice x0 -> x1, local copies, waits for them, and re-layouts: none -> 2.03 us  [per_device(): maps[:, rows:]]
    sub x1 -> x0, other arithmetic: 1.68 us -> none  [per_device(): real_part = split[:, 0, :, :3] - split[:, 1, :, 3:]]
  transfers between devices with their start and end apart: 1 -> 1, of which waited for: 1 -> 1; matrix products, arithmetic and copies ran while one was open for 0% -> 1% of each run, Pallas kernels for 0% -> 0%
where the time goes in v1:
time: 71.3 us; the launch traced here: 70.9 us
  blocking collectives  39.7 us (56%)
  local copies, waits for them, and re-layouts  10.6 us (15%)
  Pallas kernels  9.2 us (13%)
  waiting for transfers between devices  5.29 us (7%)
  starting transfers between devices  3.72 us (5%)
  other arithmetic  2.14 us (3%)
    all_gather x1, blocking collectives, per_device(): maps = lax.all_gather(local, 'site', axis=2, tiled=True)  39.7 us
    pallas_call x1, Pallas kernels, per_device(): pl.pallas_call(kernel, out_shape=jax.ShapeDtypeStruct((rupture_total * ro...  9.2 us
    unnamed x12, local copies, waits for them, and re-layouts  5.88 us
    all_to_all x1, waiting for transfers between devices, per_device(): lax.all_to_all(packed, 'fault', split_axis=0, concat_axis=0, tiled=True)  5.29 us
    all_to_all x1, starting transfers between devices, per_device(): lax.all_to_all(packed, 'fault', split_axis=0, concat_axis=0, tiled=True)  3.72 us
    slice x1, local copies, waits for them, and re-layouts, per_device(): maps[:, rows:]  2.03 us
  transfers between devices with their start and end apart: 1, of which 1 were waited for; matrix products, arithmetic and copies ran while one was open for 1% of the time, Pallas kernels for 0%

profile of v1, /device:TPU:0, one launch (start us, length us, event | category | flops | bytes accessed | tf_op | source)
XLA Modules:
  0.0 70.9 jit_solution(16943985506917254876)
XLA Ops:
  0.0 0.8 %convert_element_type.8 = f32[16,8,64]{2,1,0:T(8,128)S(1)} convert(bf16[16,8,64]{2,1,0:T(8,128)(2,1)} %param.8) | non-fusion elementwise | flops 8192 | bytes 49152 | tf_op jit(solution)/shard_map/convert_element_type | solution.py:134
  0.8 0.9 %pad_maximum_fusion = f32[16,16,64]{2,1,0:T(8,128)S(1)} fusion(f32[16,8,64]{2,1,0:T(8,128)} %param.9, f32[16,8,64]{2,1,0:T(8,128)S(1)} %convert_element_type.8), kind=kLoop, calls=%fused_computation.6 | loop fusion | flops 16384 | bytes 131072 | tf_op jit(solution)/shard_map/concatenate | solution.py:134
  1.6 0.3 copy.18
  1.9 39.7 %all_gather.3 = f32[16,16,256]{1,0,2:T(8,128)S(1)} all-gather(f32[16,16,64]{1,0,2:T(8,128)S(1)} %copy.18), channel_id=1, replica_groups=mesh['site'=4,'fault'=8] {'site'}, dimensions={2}, use_global_device_ids=true | all-gather | bytes 327680 | tf_op jit(solution)/shard_map/all_gather | solution.py:135
  41.6 2.0 %fusion.13 = (f32[16,8,256]{1,0,2:T(8,128)S(1)}, f32[16,8,256]{1,0,2:T(8,128)}) fusion(f32[16,16,256]{1,0,2:T(8,128)S(1)} %all_gather.3), kind=kLoop, calls=%fused_computation.18 | loop fusion | bytes 524288 | tf_op jit(solution)/shard_map/slice | solution.py:154
  43.6 0.0 copy-start.1
  43.6 0.0 copy-start.2
  43.6 0.0 copy-start.3
  43.6 0.0 copy-start.4
  43.6 2.5 %copy.24.amplitude = f32[16,8,256]{2,1,0:T(8,128)S(1)} copy(f32[16,8,256]{1,0,2:T(8,128)} %get-tuple-element.6) | data formatting | bytes 262144
  46.1 1.0 %copy.25.arrival = f32[16,8,256]{2,1,0:T(8,128)S(1)} copy(f32[16,8,256]{1,0,2:T(8,128)S(1)} %get-tuple-element.5) | data formatting | bytes 262144
  47.1 0.0 copy-done.1
  47.1 0.0 copy-done.2
  47.1 0.0 copy-done.3
  47.1 0.0 copy-done.4
  47.2 0.0 copy-start
  47.2 2.3 %copy-done = bf16[1,16,96,6,256]{4,2,3,1,0:T(8,128)(2,1)S(1)} copy-done((bf16[1,16,96,6,256]{4,2,3,1,0:T(8,128)(2,1)S(1)}, bf16[1,16,96,6,256]{4,2,3,1,0:T(8,128)(2,1)}, u32[]{:S(2)}) %copy-start) | copy-done | bytes 4718616
  49.5 9.2 %shard_map.73 = f32[64,768]{1,0:T(8,128)S(1)} custom-call(s32[8,16]{1,0:T(8,128)S(1)} %bitcast.15, s32[16]{0:T(128)S(1)} %copy-done.2, s32[16]{0:T(128)S(1)} %copy-done.3, s32[8]{0:T(128)S(1)} %copy-done.4, f32[16,8,256]{2,1,0:T(8,128)S(1)} %copy.24.amplitude, f32[16,8,256]{2,1,0:T(8,128)S(1)} %copy.25.arrival, bf16[16,6,96,256]{3,2,1,0:T(8,128)(2,1)S(1)} %bitcast.14), custom_call_target="tpu_custom_call" | custom-call | flops 2000000000 | bytes 5000000 | tf_op jit(solution)/shard_map/pallas_call | solution.py:139
  58.7 0.4 reshape.22
  59.1 1.2 %all_to_all.8 = f32[8,1,4608]{2,1,0:T(1,128)} reshape(f32[8,8,3,2,3,32]{5,4,3,2,1,0:T(4,128)S(1)} %bitcast.16) | data formatting | bytes 294912 | tf_op jit(solution)/shard_map/all_to_all | solution.py:159
  60.3 3.7 %all-to-all-start = ((f32[8,1,4608]{2,1,0:T(1,128)}), f32[8,1,4608]{2,1,0:T(1,128)S(1)}, u32[]{:S(2)}, u32[]{:S(2)}) async-start(f32[8,1,4608]{2,1,0:T(1,128)} %all_to_all.8), calls=%async_computation | async-start | bytes 294912 | tf_op jit(solution)/shard_map/all_to_all | solution.py:159
  64.0 0.4 sine_negate_fusion
  64.4 5.3 %all-to-all-done = f32[8,1,4608]{2,1,0:T(1,128)S(1)} async-done(((f32[8,1,4608]{2,1,0:T(1,128)}), f32[8,1,4608]{2,1,0:T(1,128)S(1)}, u32[]{:S(2)}, u32[]{:S(2)}) %all-to-all-start) | async-done | bytes 147488 | tf_op jit(solution)/shard_map/all_to_all | solution.py:159
  69.7 0.1 reduce_sum.9
  69.8 0.1 reshape.23
  69.9 0.1 reshape.24
  70.1 0.2 convolution_bitcast_fusion
  70.2 0.7 copy.23
  (1 shorter events, 0.0 us)
Async XLA Ops:
  43.6 3.5 %copy-start.1 = (s32[16,8]{0,1:T(8,128)S(1)}, s32[16,8]{0,1:T(8,128)}, u32[]{:S(2)}) copy-start(s32[16,8]{0,1:T(8,128)} %param.10) | copy-start | bytes 1540
  43.6 3.5 %copy-start.2 = (s32[16]{0:T(128)S(1)}, s32[16]{0:T(128)}, u32[]{:S(2)}) copy-start(s32[16]{0:T(128)} %count.1) | copy-start | bytes 196
  43.6 3.6 %copy-start.3 = (s32[16]{0:T(128)S(1)}, s32[16]{0:T(128)}, u32[]{:S(2)}) copy-start(s32[16]{0:T(128)} %rupture.1) | copy-start | bytes 196
  43.6 3.6 %copy-start.4 = (s32[8]{0:T(128)S(1)}, s32[8]{0:T(128)}, u32[]{:S(2)}) copy-start(s32[8]{0:T(128)} %owner.1) | copy-start | bytes 100
  47.2 2.3 %copy-start = (bf16[1,16,96,6,256]{4,2,3,1,0:T(8,128)(2,1)S(1)}, bf16[1,16,96,6,256]{4,2,3,1,0:T(8,128)(2,1)}, u32[]{:S(2)}) copy-start(bf16[1,16,96,6,256]{4,2,3,1,0:T(8,128)(2,1)} %param.7) | copy-start | bytes 14155780
  60.3 9.4 %all-to-all-start = ((f32[8,1,4608]{2,1,0:T(1,128)}), f32[8,1,4608]{2,1,0:T(1,128)S(1)}, u32[]{:S(2)}, u32[]{:S(2)}) async-start(f32[8,1,4608]{2,1,0:T(1,128)} %all_to_all.8), calls=%async_computation | async-start | bytes 294912 | tf_op jit(solution)/shard_map/all_to_all | solution.py:159

commit v2 on v1

v2 whole, which is shorter than its diff:
```python
import functools
import math

import jax
import jax.numpy as jnp
import numpy as np
from jax import lax
from jax.experimental import pallas as pl
from jax.experimental.pallas import tpu as pltpu
from jax.sharding import PartitionSpec as P

BLOCK = 32
HALF = 8
CHUNKS = 4
UNROLL = 2
MESH = pl.DeviceIdType.MESH


def inverse_table(freq_count):
    sample_count = 2 * freq_count
    wave = np.arange(freq_count)[:, None]
    sample = np.arange(sample_count)[None, :]
    angles = 2.0 * math.pi / sample_count * (wave * sample % sample_count)
    table = np.concatenate([np.cos(angles), -np.sin(angles)], axis=0) / math.sqrt(freq_count)
    return table.astype(np.float32)


def cos_sin(angle):
    x = angle - math.pi / 4
    y = x * x
    c = jnp.float32(1.0)
    s = jnp.float32(1.0)
    for n in (5, 4, 3, 2, 1):
        c = 1.0 - y * (c * (1.0 / ((2 * n - 1) * (2 * n))))
        s = 1.0 - y * (s * (1.0 / ((2 * n) * (2 * n + 1))))
    s = s * x
    root = math.sqrt(0.5)
    return root * (c - s), root * (c + s)


def turn(a, b):
    return a[0] * b[0] - a[1] * b[1], a[0] * b[1] + a[1] * b[0]


def phasor_blocks(pieces, freq_count, write):
    tables, steps, centres = [], [], []
    for amplitude, arrival in pieces:
        one = cos_sin(arrival * (2.0 * math.pi / (2 * freq_count)))
        one = (one[0], -one[1])
        powers = [None, one]
        for n in range(2, HALF + 1):
            powers.append(turn(powers[n // 2], powers[n - n // 2]))
        tables.append(powers)
        steps.append(turn(powers[HALF], powers[HALF]))
        centres.append((amplitude * powers[HALF][0], amplitude * powers[HALF][1]))
    for k in range(HALF, freq_count, 2 * HALF):
        for piece, powers in enumerate(tables):
            centre = centres[piece]
            write(k, piece, *centre)
            for n in range(1, HALF + 1):
                cc, ss = centre[0] * powers[n][0], centre[1] * powers[n][1]
                cs, sc = centre[0] * powers[n][1], centre[1] * powers[n][0]
                write(k - n, piece, cc + ss, sc - cs)
                if n < HALF:
                    write(k + n, piece, cc - ss, sc + cs)
            if k + 2 * HALF < freq_count:
                centres[piece] = turn(centre, steps[piece])


def make_phasors(amplitude, arrival, freq_count, phasor):
    rows, points = amplitude.shape
    lanes = 4 * BLOCK

    def write(k, piece, real, imag):
        both = jnp.concatenate([real, imag], axis=0).astype(jnp.bfloat16)
        phasor[k * 2 * rows : (k + 1) * 2 * rows, piece * lanes : (piece + 1) * lanes] = both

    cuts = [slice(at, at + lanes) for at in range(0, points, lanes)]
    phasor_blocks([(amplitude[:, cut], arrival[:, cut]) for cut in cuts], freq_count, write)


def make_spectrum(tile, rows, green, phasor, spectrum):
    freq_count = green.shape[2]
    lanes = 4 * BLOCK
    lane = lax.broadcasted_iota(jnp.int32, (2 * rows, 2 * lanes), 1) % BLOCK
    for block in range(freq_count // BLOCK):
        own = pl.ds(block * BLOCK, BLOCK)
        weights = jnp.concatenate([green[tile, c, own, :] for c in (0, 1, 2, 2, 3, 4, 5, 5)], axis=0)
        left = phasor[block * BLOCK * 2 * rows : (block + 1) * BLOCK * 2 * rows, :]
        product = lax.dot_general(
            left, weights, (((1,), (1,)), ((), ())), preferred_element_type=jnp.float32
        )
        picked = product[: 2 * rows]
        for k in range(1, BLOCK):
            picked = jnp.where(lane == k, product[k * 2 * rows : (k + 1) * 2 * rows], picked)
        real = picked[:rows, :lanes] - picked[rows:, lanes:]
        imag = picked[:rows, lanes:] + picked[rows:, :lanes]
        target = pl.ds(pl.multiple_of(tile * rows, rows), rows)
        spectrum[target, pl.ds(2 * block * lanes, lanes)] = real
        spectrum[target, pl.ds((2 * block + 1) * lanes, lanes)] = imag


def membership(ids, count, rupture, owner, row_count, rupture_total):
    tile_total = ids.shape[1]
    wide = row_count * rupture_total
    column = lax.broadcasted_iota(jnp.int32, (row_count, wide), 1)
    slot = lax.broadcasted_iota(jnp.int32, (row_count, 1), 0)
    pieces = []
    for tile in range(tile_total):
        place = owner[rupture[tile]] * row_count
        target = jnp.where(slot < count[tile], ids[:, tile : tile + 1] + place, -1)
        pieces.append((column == target).astype(jnp.float32))
    return jnp.concatenate(pieces, axis=0).astype(jnp.bfloat16)


def split(value):
    high = value.astype(jnp.bfloat16)
    return high, (value - high.astype(jnp.float32)).astype(jnp.bfloat16)


def route_rows(member, value):
    high, low = split(value)
    return lax.dot_general(
        jnp.concatenate([member, member], axis=0),
        jnp.concatenate([high, low], axis=0),
        (((0,), (0,)), ((), ())),
        preferred_element_type=jnp.float32,
    )


def inverse(total, table, freq_count):
    lanes = 4 * BLOCK
    rows = []
    for c in range(3):
        parts = []
        for part in range(2):
            for block in range(freq_count // BLOCK):
                at = (2 * block + part) * lanes + c * BLOCK
                parts.append(total[:, at : at + BLOCK])
        rows.append(jnp.concatenate(parts, axis=1))
    return jnp.dot(
        jnp.concatenate(rows, axis=0),
        table,
        precision=lax.Precision.HIGHEST,
        preferred_element_type=jnp.float32,
    )


def kernel(
    sites, devices, ids, count, rupture, owner, slip, time, table_hbm, green_hbm, out,
    green, table, maps, phasors, spectrum, member, partial, landed,
    green_sems, table_sem, map_send, map_recv, sum_send, sum_recv,
):
    tile_total, rows, local_points = slip.shape
    freq_count = green.shape[2]
    me = lax.axis_index("site")
    mine = lax.axis_index("fault")
    barrier = pltpu.get_barrier_semaphore()

    def greet_site(step, carry):
        peer = lax.rem(me + step, sites)
        pl.semaphore_signal(barrier, inc=1, device_id={"site": peer}, device_id_type=MESH)
        return carry

    def greet_fault(step, carry):
        peer = lax.rem(mine + step, devices)
        pl.semaphore_signal(barrier, inc=1, device_id={"fault": peer}, device_id_type=MESH)
        return carry

    lax.fori_loop(1, sites, greet_site, 0)
    lax.fori_loop(1, devices, greet_fault, 0)
    for tile in range(tile_total):
        pltpu.make_async_copy(green_hbm.at[tile], green.at[tile], green_sems.at[tile]).start()
    table_copy = pltpu.make_async_copy(table_hbm, table, table_sem)
    table_copy.start()
    maps[me] = jnp.concatenate([slip[...].astype(jnp.float32), time[...]], axis=2)
    pl.semaphore_wait(barrier, sites + devices - 2)

    chunk = tile_total // CHUNKS

    def map_copy(part, step):
        tiles = pl.ds(part * chunk, chunk)
        return pltpu.make_async_remote_copy(
            src_ref=maps.at[me, tiles],
            dst_ref=maps.at[me, tiles],
            send_sem=map_send.at[part, step],
            recv_sem=map_recv.at[part, me],
            device_id={"site": lax.rem(me + step, sites)},
            device_id_type=MESH,
        )

    def map_arrival(part, step):
        source = lax.rem(me + step, sites)
        tiles = pl.ds(part * chunk, chunk)
        return pltpu.make_async_remote_copy(
            src_ref=maps.at[source, tiles],
            dst_ref=maps.at[source, tiles],
            send_sem=map_send.at[part, step],
            recv_sem=map_recv.at[part, source],
            device_id={"site": source},
            device_id_type=MESH,
        )

    def over(first, last, body):
        lax.fori_loop(first, last, lambda step, carry: (body(step), carry)[1], 0)

    over(0, CHUNKS, lambda part: over(1, sites, lambda step: map_copy(part, step).start()))
    member[...] = membership(ids, count, rupture, owner, rows, owner.shape[0])

    def compute(part):
        over(1, sites, lambda step: map_arrival(part, step).wait_recv())

        def group(index):
            first = part * chunk + index * len(phasors)
            for at, phasor in enumerate(phasors):
                tile = first + at
                pltpu.make_async_copy(green_hbm.at[tile], green.at[tile], green_sems.at[tile]).wait()
            for at, phasor in enumerate(phasors):
                tile = first + at
                blocks = [maps[site, tile] for site in range(sites)]
                amplitude = jnp.concatenate([b[:, :local_points] for b in blocks], axis=1)
                arrival = jnp.concatenate([b[:, local_points:] for b in blocks], axis=1)
                make_phasors(amplitude, arrival, freq_count, phasor)
                make_spectrum(tile, rows, green, phasor, spectrum)

        over(0, chunk // len(phasors), group)

    over(0, CHUNKS, compute)
    routed = route_rows(member[...], spectrum[...])
    height = routed.shape[0] // devices
    for device in range(devices):
        partial[device] = routed[device * height : (device + 1) * height]

    def sum_copy(step):
        peer = lax.rem(mine + step, devices)
        return pltpu.make_async_remote_copy(
            src_ref=partial.at[peer],
            dst_ref=landed.at[mine],
            send_sem=sum_send.at[step],
            recv_sem=sum_recv.at[mine],
            device_id={"fault": peer},
            device_id_type=MESH,
        )

    def sum_arrival(step):
        source = lax.rem(mine + step, devices)
        return pltpu.make_async_remote_copy(
            src_ref=partial.at[source],
            dst_ref=landed.at[source],
            send_sem=sum_send.at[step],
            recv_sem=sum_recv.at[source],
            device_id={"fault": source},
            device_id_type=MESH,
        )

    over(1, devices, lambda step: sum_copy(step).start())
    table_copy.wait()
    total = partial[mine]
    for step in range(1, devices):
        sum_arrival(step).wait_recv()
        total = total + landed[lax.rem(mine + step, devices)]
    seismic = inverse(total, table[...], freq_count)
    for c in range(3):
        out[:, c, :] = seismic[c * height : (c + 1) * height]
    over(0, CHUNKS, lambda part: over(1, sites, lambda step: map_copy(part, step).wait_send()))
    over(1, devices, lambda step: sum_copy(step).wait_send())


def per_device(
    sites, devices,
    green_tensor, slip_map, rupture_time, variation_ids, variation_count, tile_rupture, owner_slot,
):
    green = jnp.swapaxes(green_tensor[0], 1, 2)
    tile_total, _, freq_count, points = green.shape
    rows, local_points = slip_map.shape[1:]
    rupture_total = owner_slot.shape[0]
    width = 8 * freq_count
    height = rupture_total * rows // devices
    smem = pl.BlockSpec(memory_space=pltpu.SMEM)
    vmem = pl.BlockSpec(memory_space=pltpu.VMEM)
    anywhere = pl.BlockSpec(memory_space=pl.ANY)
    dma = pltpu.SemaphoreType.DMA
    seismic = pl.pallas_call(
        functools.partial(kernel, sites, devices),
        out_shape=jax.ShapeDtypeStruct((height, 3, 2 * freq_count), jnp.float32),
        in_specs=[vmem, smem, smem, smem, vmem, vmem, anywhere, anywhere],
        out_specs=vmem,
        scratch_shapes=[
            pltpu.VMEM(green.shape, jnp.bfloat16),
            pltpu.VMEM((2 * freq_count, 2 * freq_count), jnp.float32),
            pltpu.VMEM((sites, tile_total, rows, 2 * local_points), jnp.float32),
            [pltpu.VMEM((freq_count * 2 * rows, points), jnp.bfloat16)] * UNROLL,
            pltpu.VMEM((tile_total * rows, width), jnp.float32),
            pltpu.VMEM((tile_total * rows, rupture_total * rows), jnp.bfloat16),
            pltpu.VMEM((devices, height, width), jnp.float32),
            pltpu.VMEM((devices, height, width), jnp.float32),
            dma((tile_total,)),
            dma(()),
            dma((CHUNKS, sites)),
            dma((CHUNKS, sites)),
            dma((devices,)),
            dma((devices,)),
        ],
        compiler_params=pltpu.CompilerParams(
            collective_id=0, has_side_effects=True, vmem_limit_bytes=60 * 1024 * 1024
        ),
        cost_estimate=pl.CostEstimate(flops=2 * 10**9, bytes_accessed=5 * 10**6, transcendentals=0),
    )(
        variation_ids.T, variation_count, tile_rupture, owner_slot,
        slip_map, rupture_time, inverse_table(freq_count), green,
    )
    return seismic.reshape(rupture_total // devices, rows, 1, 3, 2 * freq_count)


def solution(mesh):
    placed = (
        P("site", "fault", None, None, None),
        P("fault", None, "site"),
        P("fault", None, "site"),
        P("fault", None),
        P("fault"),
        P("fault"),
        P(),
    )
    return jax.shard_map(
        functools.partial(per_device, mesh.shape["site"], mesh.shape["fault"]),
        mesh=mesh,
        in_specs=placed,
        out_specs=P("fault", None, "site", None, None),
        check_vma=False,
    )
```

time: 71.3 us -> 24.5 us (0.34)
  blocking collectives: 39.7 us -> 0 us
  Pallas kernels: 9.2 us -> 22.9 us
  local copies, waits for them, and re-layouts: 10.6 us -> 1.39 us
  waiting for transfers between devices: 5.29 us -> 0 us
  starting transfers between devices: 3.72 us -> 0 us
  other arithmetic: 2.14 us -> 0 us
    all_gather x1 -> x0, blocking collectives: 39.7 us -> none  [per_device(): maps = lax.all_gather(local, 'site', axis=2, tiled=True)]
    pallas_call x1, Pallas kernels: 9.2 us -> 22.9 us  [per_device(): pl.pallas_call(functools.partial(kernel, sites, devices), out_shape=jax.S...]
    unnamed x12 -> x0, local copies, waits for them, and re-layouts: 5.88 us -> none
    all_to_all x1 -> x0, waiting for transfers between devices: 5.29 us -> none  [per_device(): lax.all_to_all(packed, 'fault', split_axis=0, concat_axis=0, tiled=True)]
    all_to_all x1 -> x0, starting transfers between devices: 3.72 us -> none  [per_device(): lax.all_to_all(packed, 'fault', split_axis=0, concat_axis=0, tiled=True)]
    slice x1 -> x0, local copies, waits for them, and re-layouts: 2.03 us -> none  [per_device(): maps[:, rows:]]
    all_to_all x1 -> x0, local copies, waits for them, and re-layouts: 1.15 us -> none  [per_device(): lax.all_to_all(packed, 'fault', split_axis=0, concat_axis=0, tiled=True)]
    reshape x2 -> x1, local copies, waits for them, and re-layouts: 0.5 us -> 1.39 us  [per_device(): return seismic.reshape(rupture_total // devices, rows, 1, 3, 2 * freq_count)]
  transfers between devices with their start and end apart: 1 -> 0, of which waited for: 1 -> 0; matrix products, arithmetic and copies ran while one was open for 1% -> 0% of each run, Pallas kernels for 0% -> 0%
where the time goes in v2:
time: 24.5 us; the launch traced here: 24.3 us
  Pallas kernels  22.9 us (93%)
  local copies, waits for them, and re-layouts  1.39 us (6%)
    pallas_call x1, Pallas kernels, per_device(): pl.pallas_call(functools.partial(kernel, sites, devices), out_shape=jax.S...  22.9 us
    reshape x1, local copies, waits for them, and re-layouts, per_device(): return seismic.reshape(rupture_total // devices, rows, 1, 3, 2 * freq_count)  1.39 us

profile of v2, /device:TPU:0, one launch (start us, length us, event | category | flops | bytes accessed | tf_op | source)
XLA Modules:
  0.0 24.3 jit_solution(8495383278369030736)
XLA Ops:
  0.0 22.9 %shard_map.82 = f32[8,3,192]{2,1,0:T(4,128)} custom-call(s32[8,16]{1,0:T(8,128)} %bitcast.7, s32[16]{0:T(128)} %count.1, s32[16]{0:T(128)} %rupture.1, s32[8]{0:T(128)} %owner.1, bf16[16,8,64]{2,1,0:T(8,128)(2,1)} %slip.1, f32[16,8,64]{2,1,0:T(8,128)} %time.1, f32[192,192]{1,0:T(8,128)} %constant.2.clone.table_hbm, bf16[16,6,96,256]{3,2,1,0:T(8,128)(2,1)} %bitcast.6), custom_call_target="tpu_custom_call" | custom-call | flops 2000000000 | bytes 5000000 | tf_op jit(solution)/shard_map/pallas_call | solution.py:283
  22.9 1.4 %copy.9 = f32[1,8,1,3,192]{4,2,3,1,0:T(1,128)} copy(f32[1,8,1,3,192]{4,3,1,2,0:T(4,128)} %bitcast.5) | data formatting | bytes 36864 | tf_op jit(solution)/shard_map/reshape | solution.py:312

commit v3 on v2

--- a/solution.py
+++ b/solution.py
@@ -11,7 +11,7 @@
 
 BLOCK = 32
 HALF = 8
-CHUNKS = 4
+CHUNKS = 8
 UNROLL = 2
 MESH = pl.DeviceIdType.MESH
 
@@ -79,25 +79,33 @@
     phasor_blocks([(amplitude[:, cut], arrival[:, cut]) for cut in cuts], freq_count, write)
 
 
-def make_spectrum(tile, rows, green, phasor, spectrum):
-    freq_count = green.shape[2]
+def split(value):
+    high = value.astype(jnp.bfloat16)
+    return high, (value - high.astype(jnp.float32)).astype(jnp.bfloat16)
+
+
+def block_spectrum(tile, block, rows, green, phasor, spectrum):
     lanes = 4 * BLOCK
-    lane = lax.broadcasted_iota(jnp.int32, (2 * rows, 2 * lanes), 1) % BLOCK
-    for block in range(freq_count // BLOCK):
-        own = pl.ds(block * BLOCK, BLOCK)
-        weights = jnp.concatenate([green[tile, c, own, :] for c in (0, 1, 2, 2, 3, 4, 5, 5)], axis=0)
-        left = phasor[block * BLOCK * 2 * rows : (block + 1) * BLOCK * 2 * rows, :]
-        product = lax.dot_general(
-            left, weights, (((1,), (1,)), ((), ())), preferred_element_type=jnp.float32
-        )
-        picked = product[: 2 * rows]
-        for k in range(1, BLOCK):
-            picked = jnp.where(lane == k, product[k * 2 * rows : (k + 1) * 2 * rows], picked)
-        real = picked[:rows, :lanes] - picked[rows:, lanes:]
-        imag = picked[:rows, lanes:] + picked[rows:, :lanes]
-        target = pl.ds(pl.multiple_of(tile * rows, rows), rows)
-        spectrum[target, pl.ds(2 * block * lanes, lanes)] = real
-        spectrum[target, pl.ds((2 * block + 1) * lanes, lanes)] = imag
+    lane = lax.broadcasted_iota(jnp.int32, (rows, lanes), 1) % BLOCK
+    own = pl.ds(block * BLOCK, BLOCK)
+    weights = jnp.concatenate([green[tile, c, own, :] for c in (0, 1, 2, 2, 3, 4, 5, 5)], axis=0)
+    left = phasor[block * BLOCK * 2 * rows : (block + 1) * BLOCK * 2 * rows, :]
+    product = lax.dot_general(
+        left, weights, (((1,), (1,)), ((), ())), preferred_element_type=jnp.float32
+    )
+    picked = [None] * 4
+    for k in range(BLOCK):
+        here = lane == k
+        for quarter in range(4):
+            row, column = (2 * k + quarter // 2) * rows, quarter % 2 * lanes
+            piece = product[row : row + rows, column : column + lanes]
+            picked[quarter] = piece if k == 0 else jnp.where(here, piece, picked[quarter])
+    real_high, real_low = split(picked[0] - picked[3])
+    imag_high, imag_low = split(picked[1] + picked[2])
+    target = pl.ds(pl.multiple_of(tile * 2 * rows, 2 * rows), 2 * rows)
+    at = 2 * block * lanes
+    spectrum[target, at : at + lanes] = jnp.concatenate([real_high, real_low], axis=0)
+    spectrum[target, at + lanes : at + 2 * lanes] = jnp.concatenate([imag_high, imag_low], axis=0)
 
 
 def membership(ids, count, rupture, owner, row_count, rupture_total):
@@ -109,23 +117,12 @@
     for tile in range(tile_total):
         place = owner[rupture[tile]] * row_count
         target = jnp.where(slot < count[tile], ids[:, tile : tile + 1] + place, -1)
-        pieces.append((column == target).astype(jnp.float32))
-    return jnp.concatenate(pieces, axis=0).astype(jnp.bfloat16)
-
-
-def split(value):
-    high = value.astype(jnp.bfloat16)
-    return high, (value - high.astype(jnp.float32)).astype(jnp.bfloat16)
+        pieces += [(column == target).astype(jnp.float32)] * 2
+    return jnp.concatenate(pieces, axis=0).T.astype(jnp.bfloat16)
 
 
 def route_rows(member, value):
-    high, low = split(value)
-    return lax.dot_general(
-        jnp.concatenate([member, member], axis=0),
-        jnp.concatenate([high, low], axis=0),
-        (((0,), (0,)), ((), ())),
-        preferred_element_type=jnp.float32,
-    )
+    return jnp.dot(member, value, preferred_element_type=jnp.float32)
 
 
 def inverse(total, table, freq_count):
@@ -147,9 +144,11 @@
 
 
 def kernel(
-    sites, devices, ids, count, rupture, owner, slip, time, table_hbm, green_hbm, out,
-    green, table, maps, phasors, spectrum, member, partial, landed,
-    green_sems, table_sem, map_send, map_recv, sum_send, sum_recv,
+    sites, devices,
+    ids_hbm, count_hbm, rupture_hbm, owner_hbm, slip_hbm, time_hbm, table_hbm, green_hbm, out,
+    ids, count, rupture, owner, slip, time, table, green,
+    maps, phasors, spectrum, member, partial, landed,
+    small_sems, green_sems, map_send, map_recv, sum_send, sum_recv,
 ):
     tile_total, rows, local_points = slip.shape
     freq_count = green.shape[2]
@@ -169,10 +168,18 @@
 
     lax.fori_loop(1, sites, greet_site, 0)
     lax.fori_loop(1, devices, greet_fault, 0)
+    pairs = (
+        (slip_hbm, slip), (time_hbm, time), (ids_hbm, ids), (count_hbm, count),
+        (rupture_hbm, rupture), (owner_hbm, owner), (table_hbm, table),
+    )
+    small = [pltpu.make_async_copy(a, b, small_sems.at[i]) for i, (a, b) in enumerate(pairs)]
+    for copy in small[:-1]:
+        copy.start()
     for tile in range(tile_total):
         pltpu.make_async_copy(green_hbm.at[tile], green.at[tile], green_sems.at[tile]).start()
-    table_copy = pltpu.make_async_copy(table_hbm, table, table_sem)
-    table_copy.start()
+    small[-1].start()
+    for copy in small[:2]:
+        copy.wait()
     maps[me] = jnp.concatenate([slip[...].astype(jnp.float32), time[...]], axis=2)
     pl.semaphore_wait(barrier, sites + devices - 2)
 
@@ -205,6 +212,8 @@
         lax.fori_loop(first, last, lambda step, carry: (body(step), carry)[1], 0)
 
     over(0, CHUNKS, lambda part: over(1, sites, lambda step: map_copy(part, step).start()))
+    for copy in small[2:-1]:
+        copy.wait()
     member[...] = membership(ids, count, rupture, owner, rows, owner.shape[0])
 
     def compute(part):
@@ -221,7 +230,8 @@
                 amplitude = jnp.concatenate([b[:, :local_points] for b in blocks], axis=1)
                 arrival = jnp.concatenate([b[:, local_points:] for b in blocks], axis=1)
                 make_phasors(amplitude, arrival, freq_count, phasor)
-                make_spectrum(tile, rows, green, phasor, spectrum)
+                for block in range(freq_count // BLOCK):
+                    block_spectrum(tile, block, rows, green, phasor, spectrum)
 
         over(0, chunk // len(phasors), group)
 
@@ -254,14 +264,16 @@
         )
 
     over(1, devices, lambda step: sum_copy(step).start())
-    table_copy.wait()
+    small[-1].wait()
     total = partial[mine]
     for step in range(1, devices):
         sum_arrival(step).wait_recv()
         total = total + landed[lax.rem(mine + step, devices)]
     seismic = inverse(total, table[...], freq_count)
     for c in range(3):
-        out[:, c, :] = seismic[c * height : (c + 1) * height]
+        for row in range(height):
+            at = c * height + row
+            out[row, c] = seismic[at : at + 1]
     over(0, CHUNKS, lambda part: over(1, sites, lambda step: map_copy(part, step).wait_send()))
     over(1, devices, lambda step: sum_copy(step).wait_send())
 
@@ -276,26 +288,31 @@
     rupture_total = owner_slot.shape[0]
     width = 8 * freq_count
     height = rupture_total * rows // devices
-    smem = pl.BlockSpec(memory_space=pltpu.SMEM)
     vmem = pl.BlockSpec(memory_space=pltpu.VMEM)
     anywhere = pl.BlockSpec(memory_space=pl.ANY)
     dma = pltpu.SemaphoreType.DMA
     seismic = pl.pallas_call(
         functools.partial(kernel, sites, devices),
-        out_shape=jax.ShapeDtypeStruct((height, 3, 2 * freq_count), jnp.float32),
-        in_specs=[vmem, smem, smem, smem, vmem, vmem, anywhere, anywhere],
+        out_shape=jax.ShapeDtypeStruct((height, 3, 1, 2 * freq_count), jnp.float32),
+        in_specs=[anywhere] * 8,
         out_specs=vmem,
         scratch_shapes=[
+            pltpu.VMEM((rows, tile_total), jnp.int32),
+            pltpu.SMEM((tile_total,), jnp.int32),
+            pltpu.SMEM((tile_total,), jnp.int32),
+            pltpu.SMEM((rupture_total,), jnp.int32),
+            pltpu.VMEM(slip_map.shape, slip_map.dtype),
+            pltpu.VMEM(rupture_time.shape, jnp.float32),
+            pltpu.VMEM((2 * freq_count, 2 * freq_count), jnp.float32),
             pltpu.VMEM(green.shape, jnp.bfloat16),
-            pltpu.VMEM((2 * freq_count, 2 * freq_count), jnp.float32),
             pltpu.VMEM((sites, tile_total, rows, 2 * local_points), jnp.float32),
             [pltpu.VMEM((freq_count * 2 * rows, points), jnp.bfloat16)] * UNROLL,
-            pltpu.VMEM((tile_total * rows, width), jnp.float32),
-            pltpu.VMEM((tile_total * rows, rupture_total * rows), jnp.bfloat16),
+            pltpu.VMEM((tile_total * 2 * rows, width), jnp.bfloat16),
+            pltpu.VMEM((rupture_total * rows, tile_total * 2 * rows), jnp.bfloat16),
             pltpu.VMEM((devices, height, width), jnp.float32),
             pltpu.VMEM((devices, height, width), jnp.float32),
+            dma((7,)),
             dma((tile_total,)),
-            dma(()),
             dma((CHUNKS, sites)),
             dma((CHUNKS, sites)),
             dma((devices,)),
@@ -309,7 +326,8 @@
         variation_ids.T, variation_count, tile_rupture, owner_slot,
         slip_map, rupture_time, inverse_table(freq_count), green,
     )
-    return seismic.reshape(rupture_total // devices, rows, 1, 3, 2 * freq_count)
+    seismic = seismic.reshape(rupture_total // devices, rows, 3, 1, 2 * freq_count)
+    return jnp.swapaxes(seismic, 2, 3)
 
 
 def solution(mesh):

time: 24.5 us -> 24 us (0.980)
  Pallas kernels: 22.9 us -> 22.4 us
    reshape x1 -> x0, local copies, waits for them, and re-layouts: 1.39 us -> none  [per_device(): return seismic.reshape(rupture_total // devices, rows, 1, 3, 2 * freq_count)]
    unnamed x0 -> x1, local copies, waits for them, and re-layouts: none -> 1.35 us
    pallas_call x1, Pallas kernels: 22.9 us -> 22.4 us  [per_device(): pl.pallas_call(functools.partial(kernel, sites, devices), out_shape=jax.S...]
where the time goes in v3:
time: 24 us; the launch traced here: 23.8 us
  Pallas kernels  22.4 us (93%)
  local copies, waits for them, and re-layouts  1.35 us (6%)
    pallas_call x1, Pallas kernels, per_device(): pl.pallas_call(functools.partial(kernel, sites, devices), out_shape=jax.S...  22.4 us
    unnamed x1, local copies, waits for them, and re-layouts  1.35 us

profile of v3, /device:TPU:0, one launch (start us, length us, event | category | flops | bytes accessed | tf_op | source)
XLA Modules:
  0.0 23.8 jit_solution(4464307852223630423)
XLA Ops:
  0.0 22.4 %shard_map.82 = f32[8,3,1,192]{3,2,1,0:T(1,128)} custom-call(s32[8,16]{1,0:T(8,128)} %bitcast.9, s32[16]{0:T(128)} %count_hbm.1, s32[16]{0:T(128)} %rupture_hbm.1, s32[8]{0:T(128)} %owner_hbm.1, bf16[16,8,64]{2,1,0:T(8,128)(2,1)} %slip_hbm.1, f32[16,8,64]{2,1,0:T(8,128)} %time_hbm.1, f32[192,192]{1,0:T(8,128)} %constant.2.clone.table_hbm, ...), custom_call_target="tpu_custom_call" | custom-call | flops 2000000000 | bytes 5000000 | tf_op jit(solution)/shard_map/pallas_call | solution.py:294
  22.4 1.4 %copy.11 = f32[1,8,1,3,192]{4,2,3,1,0:T(1,128)} copy(f32[1,8,1,3,192]{4,2,3,1,0:T(1,128)} %bitcast.7) | data formatting | bytes 36864

commit v4 on v3

--- a/solution.py
+++ b/solution.py
@@ -11,8 +11,7 @@
 
 BLOCK = 32
 HALF = 8
-CHUNKS = 8
-UNROLL = 2
+CHUNK = 2
 MESH = pl.DeviceIdType.MESH
 
 
@@ -65,6 +64,7 @@
                     write(k + n, piece, cc - ss, sc + cs)
             if k + 2 * HALF < freq_count:
                 centres[piece] = turn(centre, steps[piece])
+        yield
 
 
 def make_phasors(amplitude, arrival, freq_count, phasor):
@@ -76,7 +76,7 @@
         phasor[k * 2 * rows : (k + 1) * 2 * rows, piece * lanes : (piece + 1) * lanes] = both
 
     cuts = [slice(at, at + lanes) for at in range(0, points, lanes)]
-    phasor_blocks([(amplitude[:, cut], arrival[:, cut]) for cut in cuts], freq_count, write)
+    return phasor_blocks([(amplitude[:, cut], arrival[:, cut]) for cut in cuts], freq_count, write)
 
 
 def split(value):
@@ -183,7 +183,8 @@
     maps[me] = jnp.concatenate([slip[...].astype(jnp.float32), time[...]], axis=2)
     pl.semaphore_wait(barrier, sites + devices - 2)
 
-    chunk = tile_total // CHUNKS
+    chunk = CHUNK
+    chunks = tile_total // CHUNK
 
     def map_copy(part, step):
         tiles = pl.ds(part * chunk, chunk)
@@ -211,31 +212,43 @@
     def over(first, last, body):
         lax.fori_loop(first, last, lambda step, carry: (body(step), carry)[1], 0)
 
-    over(0, CHUNKS, lambda part: over(1, sites, lambda step: map_copy(part, step).start()))
+    over(0, chunks, lambda part: over(1, sites, lambda step: map_copy(part, step).start()))
     for copy in small[2:-1]:
         copy.wait()
     member[...] = membership(ids, count, rupture, owner, rows, owner.shape[0])
 
-    def compute(part):
+    def arrive(part):
         over(1, sites, lambda step: map_arrival(part, step).wait_recv())
 
-        def group(index):
-            first = part * chunk + index * len(phasors)
-            for at, phasor in enumerate(phasors):
-                tile = first + at
-                pltpu.make_async_copy(green_hbm.at[tile], green.at[tile], green_sems.at[tile]).wait()
-            for at, phasor in enumerate(phasors):
-                tile = first + at
-                blocks = [maps[site, tile] for site in range(sites)]
-                amplitude = jnp.concatenate([b[:, :local_points] for b in blocks], axis=1)
-                arrival = jnp.concatenate([b[:, local_points:] for b in blocks], axis=1)
-                make_phasors(amplitude, arrival, freq_count, phasor)
-                for block in range(freq_count // BLOCK):
-                    block_spectrum(tile, block, rows, green, phasor, spectrum)
-
-        over(0, chunk // len(phasors), group)
-
-    over(0, CHUNKS, compute)
+    def phasor_steps(tile, phasor):
+        blocks = [maps[site, tile] for site in range(sites)]
+        amplitude = jnp.concatenate([b[:, :local_points] for b in blocks], axis=1)
+        arrival = jnp.concatenate([b[:, local_points:] for b in blocks], axis=1)
+        return make_phasors(amplitude, arrival, freq_count, phasor)
+
+    def dot_steps(tile, phasor):
+        pltpu.make_async_copy(green_hbm.at[tile], green.at[tile], green_sems.at[tile]).wait()
+        for block in range(freq_count // BLOCK):
+            yield
+            block_spectrum(tile, block, rows, green, phasor, spectrum)
+
+    def alternate(*works):
+        works = list(works)
+        while works:
+            works = [work for work in works if next(work, works) is not works]
+
+    def pair(index):
+        first = index * chunk
+        alternate(dot_steps(first, phasors[0]), phasor_steps(first + 1, phasors[1]))
+        arrive(index + 1)
+        alternate(dot_steps(first + 1, phasors[1]), phasor_steps(first + 2, phasors[0]))
+
+    arrive(0)
+    alternate(phasor_steps(0, phasors[0]))
+    over(0, chunks - 1, pair)
+    last = tile_total - 2
+    alternate(dot_steps(last, phasors[0]), phasor_steps(last + 1, phasors[1]))
+    alternate(dot_steps(last + 1, phasors[1]))
     routed = route_rows(member[...], spectrum[...])
     height = routed.shape[0] // devices
     for device in range(devices):
@@ -274,7 +287,7 @@
         for row in range(height):
             at = c * height + row
             out[row, c] = seismic[at : at + 1]
-    over(0, CHUNKS, lambda part: over(1, sites, lambda step: map_copy(part, step).wait_send()))
+    over(0, chunks, lambda part: over(1, sites, lambda step: map_copy(part, step).wait_send()))
     over(1, devices, lambda step: sum_copy(step).wait_send())
 
 
@@ -306,15 +319,15 @@
             pltpu.VMEM((2 * freq_count, 2 * freq_count), jnp.float32),
             pltpu.VMEM(green.shape, jnp.bfloat16),
             pltpu.VMEM((sites, tile_total, rows, 2 * local_points), jnp.float32),
-            [pltpu.VMEM((freq_count * 2 * rows, points), jnp.bfloat16)] * UNROLL,
+            [pltpu.VMEM((freq_count * 2 * rows, points), jnp.bfloat16)] * 2,
             pltpu.VMEM((tile_total * 2 * rows, width), jnp.bfloat16),
             pltpu.VMEM((rupture_total * rows, tile_total * 2 * rows), jnp.bfloat16),
             pltpu.VMEM((devices, height, width), jnp.float32),
             pltpu.VMEM((devices, height, width), jnp.float32),
             dma((7,)),
             dma((tile_total,)),
-            dma((CHUNKS, sites)),
-            dma((CHUNKS, sites)),
+            dma((tile_total // CHUNK, sites)),
+            dma((tile_total // CHUNK, sites)),
             dma((devices,)),
             dma((devices,)),
         ],

time: 24 us -> 26.1 us (1.088)
  Pallas kernels: 22.4 us -> 24.6 us
    pallas_call x1, Pallas kernels: 22.4 us -> 24.6 us  [per_device(): pl.pallas_call(functools.partial(kernel, sites, devices), out_shape=jax.S...]
where the time goes in v4:
time: 26.1 us; the launch traced here: 26 us
  Pallas kernels  24.6 us (94%)
  local copies, waits for them, and re-layouts  1.35 us (5%)
    pallas_call x1, Pallas kernels, per_device(): pl.pallas_call(functools.partial(kernel, sites, devices), out_shape=jax.S...  24.6 us
    unnamed x1, local copies, waits for them, and re-layouts  1.35 us

profile of v4, /device:TPU:0, one launch (start us, length us, event | category | flops | bytes accessed | tf_op | source)
XLA Modules:
  0.0 26.0 jit_solution(8604452559016918157)
XLA Ops:
  0.0 24.6 %shard_map.82 = f32[8,3,1,192]{3,2,1,0:T(1,128)} custom-call(s32[8,16]{1,0:T(8,128)} %bitcast.9, s32[16]{0:T(128)} %count_hbm.1, s32[16]{0:T(128)} %rupture_hbm.1, s32[8]{0:T(128)} %owner_hbm.1, bf16[16,8,64]{2,1,0:T(8,128)(2,1)} %slip_hbm.1, f32[16,8,64]{2,1,0:T(8,128)} %time_hbm.1, f32[192,192]{1,0:T(8,128)} %constant.2.clone.table_hbm, ...), custom_call_target="tpu_custom_call" | custom-call | flops 2000000000 | bytes 5000000 | tf_op jit(solution)/shard_map/pallas_call | solution.py:307
  24.6 1.4 %copy.11 = f32[1,8,1,3,192]{4,2,3,1,0:T(1,128)} copy(f32[1,8,1,3,192]{4,2,3,1,0:T(1,128)} %bitcast.7) | data formatting | bytes 36864

commit v5 on v3

--- a/solution.py
+++ b/solution.py
@@ -42,41 +42,46 @@
     return a[0] * b[0] - a[1] * b[1], a[0] * b[1] + a[1] * b[0]
 
 
-def phasor_blocks(pieces, freq_count, write):
-    tables, steps, centres = [], [], []
-    for amplitude, arrival in pieces:
-        one = cos_sin(arrival * (2.0 * math.pi / (2 * freq_count)))
-        one = (one[0], -one[1])
-        powers = [None, one]
-        for n in range(2, HALF + 1):
-            powers.append(turn(powers[n // 2], powers[n - n // 2]))
-        tables.append(powers)
-        steps.append(turn(powers[HALF], powers[HALF]))
-        centres.append((amplitude * powers[HALF][0], amplitude * powers[HALF][1]))
+def phasor_blocks(amplitude, arrival, freq_count, write):
+    one = cos_sin(arrival * (2.0 * math.pi / (2 * freq_count)))
+    one = (one[0], -one[1])
+    powers = [None, one]
+    for n in range(2, HALF + 1):
+        powers.append(turn(powers[n // 2], powers[n - n // 2]))
+    step = turn(powers[HALF], powers[HALF])
+    centre = (amplitude * powers[HALF][0], amplitude * powers[HALF][1])
     for k in range(HALF, freq_count, 2 * HALF):
-        for piece, powers in enumerate(tables):
-            centre = centres[piece]
-            write(k, piece, *centre)
-            for n in range(1, HALF + 1):
-                cc, ss = centre[0] * powers[n][0], centre[1] * powers[n][1]
-                cs, sc = centre[0] * powers[n][1], centre[1] * powers[n][0]
-                write(k - n, piece, cc + ss, sc - cs)
-                if n < HALF:
-                    write(k + n, piece, cc - ss, sc + cs)
-            if k + 2 * HALF < freq_count:
-                centres[piece] = turn(centre, steps[piece])
+        for n in range(1, HALF + 1):
+            cc, ss = centre[0] * powers[n][0], centre[1] * powers[n][1]
+            cs, sc = centre[0] * powers[n][1], centre[1] * powers[n][0]
+            upper = (cc - ss, sc + cs) if n < HALF else centre
+            write(k, n, ((cc + ss, sc - cs), upper))
+        if k + 2 * HALF < freq_count:
+            centre = turn(centre, step)
+
+
+def frequency_order(block):
+    order = []
+    for k in range(block * BLOCK + HALF, (block + 1) * BLOCK, 2 * HALF):
+        for n in range(1, HALF + 1):
+            order += [k - n, k + n if n < HALF else k]
+    return order
 
 
 def make_phasors(amplitude, arrival, freq_count, phasor):
     rows, points = amplitude.shape
     lanes = 4 * BLOCK
-
-    def write(k, piece, real, imag):
-        both = jnp.concatenate([real, imag], axis=0).astype(jnp.bfloat16)
-        phasor[k * 2 * rows : (k + 1) * 2 * rows, piece * lanes : (piece + 1) * lanes] = both
-
-    cuts = [slice(at, at + lanes) for at in range(0, points, lanes)]
-    phasor_blocks([(amplitude[:, cut], arrival[:, cut]) for cut in cuts], freq_count, write)
+    for start in range(0, points, lanes):
+
+        def write(k, n, values):
+            row = (k - HALF + 2 * (n - 1)) * rows
+            for part in range(2):
+                both = jnp.concatenate([values[0][part], values[1][part]], axis=0)
+                at = part * points + start
+                phasor[row : row + 2 * rows, at : at + lanes] = both.astype(jnp.bfloat16)
+
+        cut = slice(start, start + lanes)
+        phasor_blocks(amplitude[:, cut], arrival[:, cut], freq_count, write)
 
 
 def split(value):
@@ -88,20 +93,27 @@
     lanes = 4 * BLOCK
     lane = lax.broadcasted_iota(jnp.int32, (rows, lanes), 1) % BLOCK
     own = pl.ds(block * BLOCK, BLOCK)
-    weights = jnp.concatenate([green[tile, c, own, :] for c in (0, 1, 2, 2, 3, 4, 5, 5)], axis=0)
-    left = phasor[block * BLOCK * 2 * rows : (block + 1) * BLOCK * 2 * rows, :]
+    real = [green[tile, c, own, :] for c in (0, 1, 2, 2)]
+    imag = [green[tile, c, own, :] for c in (3, 4, 5, 5)]
+    weights = jnp.concatenate(
+        [
+            jnp.concatenate(real + imag, axis=0),
+            jnp.concatenate([-g for g in imag] + real, axis=0),
+        ],
+        axis=1,
+    )
+    left = phasor[block * BLOCK * rows : (block + 1) * BLOCK * rows, :]
     product = lax.dot_general(
         left, weights, (((1,), (1,)), ((), ())), preferred_element_type=jnp.float32
     )
-    picked = [None] * 4
-    for k in range(BLOCK):
-        here = lane == k
-        for quarter in range(4):
-            row, column = (2 * k + quarter // 2) * rows, quarter % 2 * lanes
-            piece = product[row : row + rows, column : column + lanes]
-            picked[quarter] = piece if k == 0 else jnp.where(here, piece, picked[quarter])
-    real_high, real_low = split(picked[0] - picked[3])
-    imag_high, imag_low = split(picked[1] + picked[2])
+    picked = [None] * 2
+    for place, k in enumerate(frequency_order(block)):
+        here = lane == k % BLOCK
+        for part in range(2):
+            piece = product[place * rows : (place + 1) * rows, part * lanes : (part + 1) * lanes]
+            picked[part] = piece if place == 0 else jnp.where(here, piece, picked[part])
+    real_high, real_low = split(picked[0])
+    imag_high, imag_low = split(picked[1])
     target = pl.ds(pl.multiple_of(tile * 2 * rows, 2 * rows), 2 * rows)
     at = 2 * block * lanes
     spectrum[target, at : at + lanes] = jnp.concatenate([real_high, real_low], axis=0)
@@ -306,7 +318,7 @@
             pltpu.VMEM((2 * freq_count, 2 * freq_count), jnp.float32),
             pltpu.VMEM(green.shape, jnp.bfloat16),
             pltpu.VMEM((sites, tile_total, rows, 2 * local_points), jnp.float32),
-            [pltpu.VMEM((freq_count * 2 * rows, points), jnp.bfloat16)] * UNROLL,
+            [pltpu.VMEM((freq_count * rows, 2 * points), jnp.bfloat16)] * UNROLL,
             pltpu.VMEM((tile_total * 2 * rows, width), jnp.bfloat16),
             pltpu.VMEM((rupture_total * rows, tile_total * 2 * rows), jnp.bfloat16),
             pltpu.VMEM((devices, height, width), jnp.float32),

time: 24 us -> 23.7 us (0.987)
  Pallas kernels: 22.4 us -> 22.1 us
    pallas_call x1, Pallas kernels: 22.4 us -> 22.1 us  [per_device(): pl.pallas_call(functools.partial(kernel, sites, devices), out_shape=jax.S...]
where the time goes in v5:
time: 23.7 us; the launch traced here: 23.5 us
  Pallas kernels  22.1 us (93%)
  local copies, waits for them, and re-layouts  1.35 us (6%)
    pallas_call x1, Pallas kernels, per_device(): pl.pallas_call(functools.partial(kernel, sites, devices), out_shape=jax.S...  22.1 us
    unnamed x1, local copies, waits for them, and re-layouts  1.35 us

profile of v5, /device:TPU:0, one launch (start us, length us, event | category | flops | bytes accessed | tf_op | source)
XLA Modules:
  0.0 23.5 jit_solution(9565437133460845508)
XLA Ops:
  0.0 22.1 %shard_map.82 = f32[8,3,1,192]{3,2,1,0:T(1,128)} custom-call(s32[8,16]{1,0:T(8,128)} %bitcast.9, s32[16]{0:T(128)} %count_hbm.1, s32[16]{0:T(128)} %rupture_hbm.1, s32[8]{0:T(128)} %owner_hbm.1, bf16[16,8,64]{2,1,0:T(8,128)(2,1)} %slip_hbm.1, f32[16,8,64]{2,1,0:T(8,128)} %time_hbm.1, f32[192,192]{1,0:T(8,128)} %constant.2.clone.table_hbm, ...), custom_call_target="tpu_custom_call" | custom-call | flops 2000000000 | bytes 5000000 | tf_op jit(solution)/shard_map/pallas_call | solution.py:306
  22.1 1.4 %copy.11 = f32[1,8,1,3,192]{4,2,3,1,0:T(1,128)} copy(f32[1,8,1,3,192]{4,2,3,1,0:T(1,128)} %bitcast.7) | data formatting | bytes 36864

commit v6 on v5

--- a/solution.py
+++ b/solution.py
@@ -12,6 +12,7 @@
 BLOCK = 32
 HALF = 8
 CHUNKS = 8
+AHEAD = 2
 UNROLL = 2
 MESH = pl.DeviceIdType.MESH
 
@@ -137,28 +138,19 @@
     return jnp.dot(member, value, preferred_element_type=jnp.float32)
 
 
-def inverse(total, table, freq_count):
-    lanes = 4 * BLOCK
-    rows = []
-    for c in range(3):
-        parts = []
-        for part in range(2):
-            for block in range(freq_count // BLOCK):
-                at = (2 * block + part) * lanes + c * BLOCK
-                parts.append(total[:, at : at + BLOCK])
-        rows.append(jnp.concatenate(parts, axis=1))
-    return jnp.dot(
-        jnp.concatenate(rows, axis=0),
-        table,
-        precision=lax.Precision.HIGHEST,
-        preferred_element_type=jnp.float32,
-    )
+def component_rows(total, c, freq_count):
+    parts = []
+    for part in range(2):
+        for block in range(freq_count // BLOCK):
+            at = ((2 * block + part) * 3 + c) * BLOCK
+            parts.append(total[:, at : at + BLOCK])
+    return jnp.concatenate(parts, axis=1)
 
 
 def kernel(
     sites, devices,
-    ids_hbm, count_hbm, rupture_hbm, owner_hbm, slip_hbm, time_hbm, table_hbm, green_hbm, out,
-    ids, count, rupture, owner, slip, time, table, green,
+    ids_hbm, count_hbm, rupture_hbm, owner_hbm, slip_hbm, time_hbm, green_hbm, out,
+    ids, count, rupture, owner, slip, time, green,
     maps, phasors, spectrum, member, partial, landed,
     small_sems, green_sems, map_send, map_recv, sum_send, sum_recv,
 ):
@@ -182,14 +174,13 @@
     lax.fori_loop(1, devices, greet_fault, 0)
     pairs = (
         (slip_hbm, slip), (time_hbm, time), (ids_hbm, ids), (count_hbm, count),
-        (rupture_hbm, rupture), (owner_hbm, owner), (table_hbm, table),
+        (rupture_hbm, rupture), (owner_hbm, owner),
     )
     small = [pltpu.make_async_copy(a, b, small_sems.at[i]) for i, (a, b) in enumerate(pairs)]
-    for copy in small[:-1]:
+    for copy in small:
         copy.start()
     for tile in range(tile_total):
         pltpu.make_async_copy(green_hbm.at[tile], green.at[tile], green_sems.at[tile]).start()
-    small[-1].start()
     for copy in small[:2]:
         copy.wait()
     maps[me] = jnp.concatenate([slip[...].astype(jnp.float32), time[...]], axis=2)
@@ -223,13 +214,21 @@
     def over(first, last, body):
         lax.fori_loop(first, last, lambda step, carry: (body(step), carry)[1], 0)
 
-    over(0, CHUNKS, lambda part: over(1, sites, lambda step: map_copy(part, step).start()))
-    for copy in small[2:-1]:
+    def send(part):
+        over(1, sites, lambda step: map_copy(part, step).start())
+
+    over(0, AHEAD, send)
+    for copy in small[2:]:
         copy.wait()
     member[...] = membership(ids, count, rupture, owner, rows, owner.shape[0])
 
     def compute(part):
         over(1, sites, lambda step: map_arrival(part, step).wait_recv())
+
+        @pl.when(part + AHEAD < CHUNKS)
+        def _():
+            send(part + AHEAD)
+
 
         def group(index):
             first = part * chunk + index * len(phasors)
@@ -249,6 +248,10 @@
 
     over(0, CHUNKS, compute)
     routed = route_rows(member[...], spectrum[...])
+    lanes = 4 * BLOCK
+    routed = jnp.concatenate(
+        [routed[:, at : at + 3 * BLOCK] for at in range(0, routed.shape[1], lanes)], axis=1
+    )
     height = routed.shape[0] // devices
     for device in range(devices):
         partial[device] = routed[device * height : (device + 1) * height]
@@ -276,16 +279,14 @@
         )
 
     over(1, devices, lambda step: sum_copy(step).start())
-    small[-1].wait()
     total = partial[mine]
     for step in range(1, devices):
         sum_arrival(step).wait_recv()
         total = total + landed[lax.rem(mine + step, devices)]
-    seismic = inverse(total, table[...], freq_count)
     for c in range(3):
+        found = component_rows(total, c, freq_count)
         for row in range(height):
-            at = c * height + row
-            out[row, c] = seismic[at : at + 1]
+            out[3 * row + c : 3 * row + c + 1, :] = found[row : row + 1]
     over(0, CHUNKS, lambda part: over(1, sites, lambda step: map_copy(part, step).wait_send()))
     over(1, devices, lambda step: sum_copy(step).wait_send())
 
@@ -303,10 +304,10 @@
     vmem = pl.BlockSpec(memory_space=pltpu.VMEM)
     anywhere = pl.BlockSpec(memory_space=pl.ANY)
     dma = pltpu.SemaphoreType.DMA
-    seismic = pl.pallas_call(
+    owned = pl.pallas_call(
         functools.partial(kernel, sites, devices),
-        out_shape=jax.ShapeDtypeStruct((height, 3, 1, 2 * freq_count), jnp.float32),
-        in_specs=[anywhere] * 8,
+        out_shape=jax.ShapeDtypeStruct((height * 3, 2 * freq_count), jnp.float32),
+        in_specs=[anywhere] * 7,
         out_specs=vmem,
         scratch_shapes=[
             pltpu.VMEM((rows, tile_total), jnp.int32),
@@ -315,15 +316,14 @@
             pltpu.SMEM((rupture_total,), jnp.int32),
             pltpu.VMEM(slip_map.shape, slip_map.dtype),
             pltpu.VMEM(rupture_time.shape, jnp.float32),
-            pltpu.VMEM((2 * freq_count, 2 * freq_count), jnp.float32),
             pltpu.VMEM(green.shape, jnp.bfloat16),
             pltpu.VMEM((sites, tile_total, rows, 2 * local_points), jnp.float32),
             [pltpu.VMEM((freq_count * rows, 2 * points), jnp.bfloat16)] * UNROLL,
             pltpu.VMEM((tile_total * 2 * rows, width), jnp.bfloat16),
             pltpu.VMEM((rupture_total * rows, tile_total * 2 * rows), jnp.bfloat16),
-            pltpu.VMEM((devices, height, width), jnp.float32),
-            pltpu.VMEM((devices, height, width), jnp.float32),
-            dma((7,)),
+            pltpu.VMEM((devices, height, 6 * freq_count), jnp.float32),
+            pltpu.VMEM((devices, height, 6 * freq_count), jnp.float32),
+            dma((6,)),
             dma((tile_total,)),
             dma((CHUNKS, sites)),
             dma((CHUNKS, sites)),
@@ -336,10 +336,15 @@
         cost_estimate=pl.CostEstimate(flops=2 * 10**9, bytes_accessed=5 * 10**6, transcendentals=0),
     )(
         variation_ids.T, variation_count, tile_rupture, owner_slot,
-        slip_map, rupture_time, inverse_table(freq_count), green,
-    )
-    seismic = seismic.reshape(rupture_total // devices, rows, 3, 1, 2 * freq_count)
-    return jnp.swapaxes(seismic, 2, 3)
+        slip_map, rupture_time, green,
+    )
+    seismic = jnp.dot(
+        owned,
+        inverse_table(freq_count),
+        precision=lax.Precision.HIGHEST,
+        preferred_element_type=jnp.float32,
+    )
+    return seismic.reshape(rupture_total // devices, rows, 1, 3, 2 * freq_count)
 
 
 def solution(mesh):

time: 23.7 us -> 29.6 us (1.25)
  Pallas kernels: 22.1 us -> 27.8 us
  matrix products: 0 us -> 0.94 us
  local copies, waits for them, and re-layouts: 1.35 us -> 0.64 us
    pallas_call x1, Pallas kernels: 22.1 us -> 27.8 us  [per_device(): pl.pallas_call(functools.partial(kernel, sites, devices), out_shape=jax.S...]
    unnamed x1 -> x2, local copies, waits for them, and re-layouts: 1.35 us -> 0.01 us
    dot_general x0 -> x1, matrix products: none -> 0.94 us  [per_device(): jnp.dot(owned, inverse_table(freq_count), precision=lax.Precision.HIGHEST...]
    reshape x0 -> x1, local copies, waits for them, and re-layouts: none -> 0.64 us  [per_device(): return seismic.reshape(rupture_total // devices, rows, 1, 3, 2 * freq_count)]
where the time goes in v6:
time: 29.6 us; the launch traced here: 29.4 us
  Pallas kernels  27.8 us (94%)
  matrix products  0.94 us (3%)
  local copies, waits for them, and re-layouts  0.64 us (2%)
    pallas_call x1, Pallas kernels, per_device(): pl.pallas_call(functools.partial(kernel, sites, devices), out_shape=jax.S...  27.8 us
    dot_general x1, matrix products, per_device(): jnp.dot(owned, inverse_table(freq_count), precision=lax.Precision.HIGHEST...  0.94 us
    reshape x1, local copies, waits for them, and re-layouts, per_device(): return seismic.reshape(rupture_total // devices, rows, 1, 3, 2 * freq_count)  0.64 us

profile of v6, /device:TPU:0, one launch (start us, length us, event | category | flops | bytes accessed | tf_op | source)
XLA Modules:
  0.0 29.4 jit_solution(17337566597222777797)
XLA Ops:
  0.0 0.0 copy-start
  0.0 27.8 %shard_map.82 = f32[24,192]{1,0:T(8,128)} custom-call(s32[8,16]{1,0:T(8,128)} %bitcast.7, s32[16]{0:T(128)} %count_hbm.1, s32[16]{0:T(128)} %rupture_hbm.1, s32[8]{0:T(128)} %owner_hbm.1, bf16[16,8,64]{2,1,0:T(8,128)(2,1)} %slip_hbm.1, f32[16,8,64]{2,1,0:T(8,128)} %time_hbm.1, bf16[16,6,96,256]{3,2,1,0:T(8,128)(2,1)} %bitcast.6), custom_call_target="tpu_custom_call" | custom-call | flops 2000000000 | bytes 5000000 | tf_op jit(solution)/shard_map/pallas_call | solution.py:307
  27.9 0.0 copy-done
  27.9 0.9 %fusion = f32[24,192]{1,0:T(8,128)S(1)} fusion(f32[24,192]{1,0:T(8,128)} %shard_map.82, f32[192,192]{1,0:T(8,128)S(1)} %copy-done), kind=kOutput, calls=%fused_computation | convolution fusion | flops 10616832 | bytes 184320 | tf_op jit(solution)/shard_map/dot_general | solution.py:341
  28.8 0.6 %reshape.4 = f32[1,8,1,3,192]{4,2,3,1,0:T(1,128)} reshape(f32[24,192]{1,0:T(8,128)S(1)} %fusion) | data formatting | bytes 36864 | tf_op jit(solution)/shard_map/reshape | solution.py:347
Async XLA Ops:
  0.0 27.9 %copy-start = (f32[192,192]{1,0:T(8,128)S(1)}, f32[192,192]{1,0:T(8,128)}, u32[]{:S(2)}) copy-start(f32[192,192]{1,0:T(8,128)} %constant.2.clone) | copy-start | bytes 442372

commit v7 on v5

--- a/solution.py
+++ b/solution.py
@@ -11,8 +11,7 @@
 
 BLOCK = 32
 HALF = 8
-CHUNKS = 8
-UNROLL = 2
+CHUNK = 2
 MESH = pl.DeviceIdType.MESH
 
 
@@ -58,6 +57,7 @@
             write(k, n, ((cc + ss, sc - cs), upper))
         if k + 2 * HALF < freq_count:
             centre = turn(centre, step)
+        yield
 
 
 def frequency_order(block):
@@ -81,7 +81,7 @@
                 phasor[row : row + 2 * rows, at : at + lanes] = both.astype(jnp.bfloat16)
 
         cut = slice(start, start + lanes)
-        phasor_blocks(amplitude[:, cut], arrival[:, cut], freq_count, write)
+        yield from phasor_blocks(amplitude[:, cut], arrival[:, cut], freq_count, write)
 
 
 def split(value):
@@ -138,13 +138,12 @@
 
 
 def inverse(total, table, freq_count):
-    lanes = 4 * BLOCK
     rows = []
     for c in range(3):
         parts = []
         for part in range(2):
             for block in range(freq_count // BLOCK):
-                at = (2 * block + part) * lanes + c * BLOCK
+                at = ((2 * block + part) * 3 + c) * BLOCK
                 parts.append(total[:, at : at + BLOCK])
         rows.append(jnp.concatenate(parts, axis=1))
     return jnp.dot(
@@ -195,7 +194,8 @@
     maps[me] = jnp.concatenate([slip[...].astype(jnp.float32), time[...]], axis=2)
     pl.semaphore_wait(barrier, sites + devices - 2)
 
-    chunk = tile_total // CHUNKS
+    chunk = CHUNK
+    chunks = tile_total // CHUNK
 
     def map_copy(part, step):
         tiles = pl.ds(part * chunk, chunk)
@@ -223,32 +223,55 @@
     def over(first, last, body):
         lax.fori_loop(first, last, lambda step, carry: (body(step), carry)[1], 0)
 
-    over(0, CHUNKS, lambda part: over(1, sites, lambda step: map_copy(part, step).start()))
+    over(0, chunks, lambda part: over(1, sites, lambda step: map_copy(part, step).start()))
     for copy in small[2:-1]:
         copy.wait()
     member[...] = membership(ids, count, rupture, owner, rows, owner.shape[0])
 
-    def compute(part):
+    def arrive(part):
         over(1, sites, lambda step: map_arrival(part, step).wait_recv())
 
-        def group(index):
-            first = part * chunk + index * len(phasors)
-            for at, phasor in enumerate(phasors):
-                tile = first + at
-                pltpu.make_async_copy(green_hbm.at[tile], green.at[tile], green_sems.at[tile]).wait()
-            for at, phasor in enumerate(phasors):
-                tile = first + at
-                blocks = [maps[site, tile] for site in range(sites)]
-                amplitude = jnp.concatenate([b[:, :local_points] for b in blocks], axis=1)
-                arrival = jnp.concatenate([b[:, local_points:] for b in blocks], axis=1)
-                make_phasors(amplitude, arrival, freq_count, phasor)
-                for block in range(freq_count // BLOCK):
-                    block_spectrum(tile, block, rows, green, phasor, spectrum)
-
-        over(0, chunk // len(phasors), group)
-
-    over(0, CHUNKS, compute)
+    def phasor_steps(tile, phasor):
+        blocks = [maps[site, tile] for site in range(sites)]
+        amplitude = jnp.concatenate([b[:, :local_points] for b in blocks], axis=1)
+        arrival = jnp.concatenate([b[:, local_points:] for b in blocks], axis=1)
+        return make_phasors(amplitude, arrival, freq_count, phasor)
+
+    def dots_beside(tile, phasor, steps):
+        block_count = freq_count // BLOCK
+        share = -(-(2 * freq_count // (2 * HALF)) // block_count)
+        for block in range(block_count):
+            block_spectrum(tile, block, rows, green, phasor, spectrum)
+            for _ in range(share):
+                next(steps, None)
+        for _ in steps:
+            pass
+
+    def green_arrive(tile):
+        pltpu.make_async_copy(green_hbm.at[tile], green.at[tile], green_sems.at[tile]).wait()
+
+    def pair(index):
+        first = index * chunk
+        arrive(index + 1)
+        green_arrive(first)
+        green_arrive(first + 1)
+        dots_beside(first, phasors[0], phasor_steps(first + 1, phasors[1]))
+        dots_beside(first + 1, phasors[1], phasor_steps(first + 2, phasors[0]))
+
+    arrive(0)
+    for _ in phasor_steps(0, phasors[0]):
+        pass
+    over(0, chunks - 1, pair)
+    last = tile_total - 2
+    green_arrive(last)
+    green_arrive(last + 1)
+    dots_beside(last, phasors[0], phasor_steps(last + 1, phasors[1]))
+    dots_beside(last + 1, phasors[1], iter(()))
     routed = route_rows(member[...], spectrum[...])
+    lanes = 4 * BLOCK
+    routed = jnp.concatenate(
+        [routed[:, at : at + 3 * BLOCK] for at in range(0, routed.shape[1], lanes)], axis=1
+    )
     height = routed.shape[0] // devices
     for device in range(devices):
         partial[device] = routed[device * height : (device + 1) * height]
@@ -286,7 +309,7 @@
         for row in range(height):
             at = c * height + row
             out[row, c] = seismic[at : at + 1]
-    over(0, CHUNKS, lambda part: over(1, sites, lambda step: map_copy(part, step).wait_send()))
+    over(0, chunks, lambda part: over(1, sites, lambda step: map_copy(part, step).wait_send()))
     over(1, devices, lambda step: sum_copy(step).wait_send())
 
 
@@ -318,15 +341,15 @@
             pltpu.VMEM((2 * freq_count, 2 * freq_count), jnp.float32),
             pltpu.VMEM(green.shape, jnp.bfloat16),
             pltpu.VMEM((sites, tile_total, rows, 2 * local_points), jnp.float32),
-            [pltpu.VMEM((freq_count * rows, 2 * points), jnp.bfloat16)] * UNROLL,
+            [pltpu.VMEM((freq_count * rows, 2 * points), jnp.bfloat16)] * 2,
             pltpu.VMEM((tile_total * 2 * rows, width), jnp.bfloat16),
             pltpu.VMEM((rupture_total * rows, tile_total * 2 * rows), jnp.bfloat16),
-            pltpu.VMEM((devices, height, width), jnp.float32),
-            pltpu.VMEM((devices, height, width), jnp.float32),
+            pltpu.VMEM((devices, height, 6 * freq_count), jnp.float32),
+            pltpu.VMEM((devices, height, 6 * freq_count), jnp.float32),
             dma((7,)),
             dma((tile_total,)),
-            dma((CHUNKS, sites)),
-            dma((CHUNKS, sites)),
+            dma((tile_total // CHUNK, sites)),
+            dma((tile_total // CHUNK, sites)),
             dma((devices,)),
             dma((devices,)),
         ],

time: 23.7 us -> 23.6 us (level)
  no operation moved by 1% of the time
where the time goes in v7:
time: 23.6 us; the launch traced here: 23.4 us
  Pallas kernels  22.1 us (94%)
  local copies, waits for them, and re-layouts  1.35 us (6%)
    pallas_call x1, Pallas kernels, per_device(): pl.pallas_call(functools.partial(kernel, sites, devices), out_shape=jax.S...  22.1 us
    unnamed x1, local copies, waits for them, and re-layouts  1.35 us

profile of v7, /device:TPU:0, one launch (start us, length us, event | category | flops | bytes accessed | tf_op | source)
XLA Modules:
  0.0 23.4 jit_solution(11846715031134223016)
XLA Ops:
  0.0 22.1 %shard_map.82 = f32[8,3,1,192]{3,2,1,0:T(1,128)} custom-call(s32[8,16]{1,0:T(8,128)} %bitcast.9, s32[16]{0:T(128)} %count_hbm.1, s32[16]{0:T(128)} %rupture_hbm.1, s32[8]{0:T(128)} %owner_hbm.1, bf16[16,8,64]{2,1,0:T(8,128)(2,1)} %slip_hbm.1, f32[16,8,64]{2,1,0:T(8,128)} %time_hbm.1, f32[192,192]{1,0:T(8,128)} %constant.2.clone.table_hbm, ...), custom_call_target="tpu_custom_call" | custom-call | flops 2000000000 | bytes 5000000 | tf_op jit(solution)/shard_map/pallas_call | solution.py:329
  22.1 1.4 %copy.11 = f32[1,8,1,3,192]{4,2,3,1,0:T(1,128)} copy(f32[1,8,1,3,192]{4,2,3,1,0:T(1,128)} %bitcast.7) | data formatting | bytes 36864

commit v8 on v7

--- a/solution.py
+++ b/solution.py
@@ -354,7 +354,7 @@
             dma((devices,)),
         ],
         compiler_params=pltpu.CompilerParams(
-            collective_id=0, has_side_effects=True, vmem_limit_bytes=60 * 1024 * 1024
+            collective_id=0, has_side_effects=True, vmem_limit_bytes=50 * 1024 * 1024
         ),
         cost_estimate=pl.CostEstimate(flops=2 * 10**9, bytes_accessed=5 * 10**6, transcendentals=0),
     )(

time: 23.6 us -> 27.5 us (1.17)
  local copies, waits for them, and re-layouts: 1.35 us -> 5.78 us
  Pallas kernels: 22.1 us -> 21.4 us
    unnamed x1 -> x15, local copies, waits for them, and re-layouts: 1.35 us -> 5.78 us
    pallas_call x1, Pallas kernels: 22.1 us -> 21.4 us  [per_device(): pl.pallas_call(functools.partial(kernel, sites, devices), out_shape=jax.S...]
where the time goes in v8:
time: 27.5 us; the launch traced here: 27.2 us
  Pallas kernels  21.4 us (78%)
  local copies, waits for them, and re-layouts  5.78 us (21%)
    pallas_call x1, Pallas kernels, per_device(): pl.pallas_call(functools.partial(kernel, sites, devices), out_shape=jax.S...  21.4 us
    unnamed x15, local copies, waits for them, and re-layouts  5.78 us

profile of v8, /device:TPU:0, one launch (start us, length us, event | category | flops | bytes accessed | tf_op | source)
XLA Modules:
  0.0 27.2 jit_solution(4330687717274142251)
XLA Ops:
  0.0 0.0 copy-start
  0.0 0.8 %copy-done = f32[16,8,64]{2,1,0:T(8,128)S(1)} copy-done((f32[16,8,64]{2,1,0:T(8,128)S(1)}, f32[16,8,64]{2,1,0:T(8,128)}, u32[]{:S(2)}) %copy-start) | copy-done | bytes 32792
  0.8 0.0 copy-start.1
  0.8 0.8 %copy-done.1 = bf16[16,8,64]{2,1,0:T(8,128)(2,1)S(1)} copy-done((bf16[16,8,64]{2,1,0:T(8,128)(2,1)S(1)}, bf16[16,8,64]{2,1,0:T(8,128)(2,1)}, u32[]{:S(2)}) %copy-start.1) | copy-done | bytes 16408
  1.6 0.0 copy-start.2
  1.6 0.7 %copy-done.2 = s32[16,8]{0,1:T(8,128)S(1)} copy-done((s32[16,8]{0,1:T(8,128)S(1)}, s32[16,8]{0,1:T(8,128)}, u32[]{:S(2)}) %copy-start.2) | copy-done | bytes 536
  2.3 0.0 copy-start.3
  2.3 0.7 %copy-done.3 = s32[16]{0:T(128)S(1)} copy-done((s32[16]{0:T(128)S(1)}, s32[16]{0:T(128)}, u32[]{:S(2)}) %copy-start.3) | copy-done | bytes 88
  2.9 0.0 copy-start.4
  2.9 0.7 %copy-done.4 = s32[16]{0:T(128)S(1)} copy-done((s32[16]{0:T(128)S(1)}, s32[16]{0:T(128)}, u32[]{:S(2)}) %copy-start.4) | copy-done | bytes 88
  3.6 0.0 copy-start.5
  3.6 0.7 %copy-done.5 = s32[8]{0:T(128)S(1)} copy-done((s32[8]{0:T(128)S(1)}, s32[8]{0:T(128)}, u32[]{:S(2)}) %copy-start.5) | copy-done | bytes 56
  4.3 0.0 copy-start.6
  4.3 0.9 %copy-done.6 = f32[192,192]{1,0:T(8,128)S(1)} copy-done((f32[192,192]{1,0:T(8,128)S(1)}, f32[192,192]{1,0:T(8,128)}, u32[]{:S(2)}) %copy-start.6) | copy-done | bytes 147480
  5.2 21.4 %shard_map.82 = f32[8,3,1,192]{3,2,1,0:T(1,128)S(1)} custom-call(s32[8,16]{1,0:T(8,128)S(1)} %bitcast.8, s32[16]{0:T(128)S(1)} %copy-done.3, s32[16]{0:T(128)S(1)} %copy-done.4, s32[8]{0:T(128)S(1)} %copy-done.5, bf16[16,8,64]{2,1,0:T(8,128)(2,1)S(1)} %copy-done.1, f32[16,8,64]{2,1,0:T(8,128)S(1)} %copy-done, f32[192,192]{1,0:T(8,128)S(1)} %copy-done.6, ...), custom_call_target="tpu_custom_call" | custom-call | flops 2000000000 | bytes 5000000 | tf_op jit(solution)/shard_map/pallas_call | solution.py:329
  26.6 0.6 %copy.11 = f32[1,8,1,3,192]{4,2,3,1,0:T(1,128)} copy(f32[1,8,1,3,192]{4,2,3,1,0:T(1,128)S(1)} %bitcast.7) | data formatting | bytes 36864
Async XLA Ops:
  0.0 0.8 %copy-start = (f32[16,8,64]{2,1,0:T(8,128)S(1)}, f32[16,8,64]{2,1,0:T(8,128)}, u32[]{:S(2)}) copy-start(f32[16,8,64]{2,1,0:T(8,128)} %time_hbm.1) | copy-start | bytes 98308
  0.8 0.8 %copy-start.1 = (bf16[16,8,64]{2,1,0:T(8,128)(2,1)S(1)}, bf16[16,8,64]{2,1,0:T(8,128)(2,1)}, u32[]{:S(2)}) copy-start(bf16[16,8,64]{2,1,0:T(8,128)(2,1)} %slip_hbm.1) | copy-start | bytes 49156
  1.6 0.7 %copy-start.2 = (s32[16,8]{0,1:T(8,128)S(1)}, s32[16,8]{0,1:T(8,128)}, u32[]{:S(2)}) copy-start(s32[16,8]{0,1:T(8,128)} %param.11) | copy-start | bytes 1540
  2.3 0.7 %copy-start.3 = (s32[16]{0:T(128)S(1)}, s32[16]{0:T(128)}, u32[]{:S(2)}) copy-start(s32[16]{0:T(128)} %count_hbm.1) | copy-start | bytes 196
  2.9 0.7 %copy-start.4 = (s32[16]{0:T(128)S(1)}, s32[16]{0:T(128)}, u32[]{:S(2)}) copy-start(s32[16]{0:T(128)} %rupture_hbm.1) | copy-start | bytes 196
  3.6 0.7 %copy-start.5 = (s32[8]{0:T(128)S(1)}, s32[8]{0:T(128)}, u32[]{:S(2)}) copy-start(s32[8]{0:T(128)} %owner_hbm.1) | copy-start | bytes 100
  4.3 0.9 %copy-start.6 = (f32[192,192]{1,0:T(8,128)S(1)}, f32[192,192]{1,0:T(8,128)}, u32[]{:S(2)}) copy-start(f32[192,192]{1,0:T(8,128)} %constant.2.clone.table_hbm) | copy-start | bytes 442372

commit v9 on v7

--- a/solution.py
+++ b/solution.py
@@ -186,9 +186,6 @@
     small = [pltpu.make_async_copy(a, b, small_sems.at[i]) for i, (a, b) in enumerate(pairs)]
     for copy in small[:-1]:
         copy.start()
-    for tile in range(tile_total):
-        pltpu.make_async_copy(green_hbm.at[tile], green.at[tile], green_sems.at[tile]).start()
-    small[-1].start()
     for copy in small[:2]:
         copy.wait()
     maps[me] = jnp.concatenate([slip[...].astype(jnp.float32), time[...]], axis=2)
@@ -224,6 +221,9 @@
         lax.fori_loop(first, last, lambda step, carry: (body(step), carry)[1], 0)
 
     over(0, chunks, lambda part: over(1, sites, lambda step: map_copy(part, step).start()))
+    for tile in range(tile_total):
+        pltpu.make_async_copy(green_hbm.at[tile], green.at[tile], green_sems.at[tile]).start()
+    small[-1].start()
     for copy in small[2:-1]:
         copy.wait()
     member[...] = membership(ids, count, rupture, owner, rows, owner.shape[0])

time: 23.6 us -> 23.6 us (level)
  no operation moved by 1% of the time
where the time goes in v9:
time: 23.6 us; the launch traced here: 23.4 us
  Pallas kernels  22 us (93%)
  local copies, waits for them, and re-layouts  1.35 us (6%)
    pallas_call x1, Pallas kernels, per_device(): pl.pallas_call(functools.partial(kernel, sites, devices), out_shape=jax.S...  22 us
    unnamed x1, local copies, waits for them, and re-layouts  1.35 us

profile of v9, /device:TPU:0, one launch (start us, length us, event | category | flops | bytes accessed | tf_op | source)
XLA Modules:
  0.0 23.4 jit_solution(13170929793302190119)
XLA Ops:
  0.0 22.0 %shard_map.82 = f32[8,3,1,192]{3,2,1,0:T(1,128)} custom-call(s32[8,16]{1,0:T(8,128)} %bitcast.9, s32[16]{0:T(128)} %count_hbm.1, s32[16]{0:T(128)} %rupture_hbm.1, s32[8]{0:T(128)} %owner_hbm.1, bf16[16,8,64]{2,1,0:T(8,128)(2,1)} %slip_hbm.1, f32[16,8,64]{2,1,0:T(8,128)} %time_hbm.1, f32[192,192]{1,0:T(8,128)} %constant.2.clone.table_hbm, ...), custom_call_target="tpu_custom_call" | custom-call | flops 2000000000 | bytes 5000000 | tf_op jit(solution)/shard_map/pallas_call | solution.py:329
  22.0 1.4 %copy.11 = f32[1,8,1,3,192]{4,2,3,1,0:T(1,128)} copy(f32[1,8,1,3,192]{4,2,3,1,0:T(1,128)} %bitcast.7) | data formatting | bytes 36864
